TPU v7x, 256 devices: a whole 4x4x8 slice. The times are simulated.
256 devices in a mesh: seq: 64 (over x, z, y_lo), head: 4 (over y_hi, core).
Axes of the slice: x: 4, y: 4 (y_hi: 2, y_lo: 2; y = y_hi * 2 + y_lo), z: 8, core: 2. Of those that a mesh axis runs over, the one named last changes fastest.
Arguments:
- queries: bfloat16 [8192, 1536], P('seq', 'head'), may hold values from -8 to 8
- cell_types: int32 [8192], P('seq'), may hold values from 0 to 127
- promoters: int32 [8192], P('seq'), may hold values from 0 to 131071, as said below
- offsets: int32 [8192], P('seq'), may hold values from -64 to 64, as said below
- cell_embed: bfloat16 [128, 1536], P(None, 'head'), may hold values from -3 to 3
- bin_keys: bfloat16 [131072, 1536], P('seq', 'head'), may hold values from -6 to 6
- bin_values: bfloat16 [131072, 1536], P('seq', 'head'), may hold values from -6 to 6
- slopes: float32 [16], P('head'), may hold values from 1.280082e-05 to 0.05
- w_out: bfloat16 [1536, 1536], P('head'), may hold values from -0.15625 to 0.15625
Outputs:
- pooled_features: bfloat16 [8192, 1536], P('seq', 'head')
Inputs may be any that keep to these rules, and one draw needn't show every extreme that they name: `promoters`: the promoter of row r lies in bins (r // 128) * 2048 to (r // 128 + 1) * 2048 - 1; in each aligned block of 128 rows, the block's first row sits at the first of those bins and its second row at the last. `offsets`: in each aligned block of 128 rows the first row has offset -64 and the second row 64.
All inputs are finite; a program needn't handle non-finite values.
Results may differ from a plain program's by a relative error of at most 0.012.
Values may be sent and summed in bfloat16 or wider, within the bound.
No kernel may reach another device: no remote copies, remote signals or barrier semaphores. Data moves between devices by JAX's collectives and lax.ppermute only.
A program may use at most 128 MiB of HBM per device.

v0:
```python
import jax
import jax.numpy as jnp
from jax import lax
from jax.sharding import PartitionSpec as P

HEAD_DIM = 96
RADIUS = 7812
HOPS = 4


def shifted(value, axis, steps):
    count = lax.axis_size(axis)
    leading, last = (max(0, -steps), min(count, count - steps))
    return lax.ppermute(value, axis, [(source, source + steps) for source in range(leading, last)])


def attend(carried, query_rows, centres, bin_keys, bin_values, first_bin, slopes, total_bins):
    run_max, run_sum, run_out = carried
    row_count = query_rows.shape[0]
    groups = slopes.shape[0]
    key_count = bin_keys.shape[0]
    query_heads = query_rows.reshape(row_count, groups, HEAD_DIM)
    key_heads = bin_keys.reshape(key_count, groups, HEAD_DIM)
    value_heads = bin_values.reshape(key_count, groups, HEAD_DIM)
    scores = jnp.einsum(
        "qgd,kgd->gqk", query_heads, key_heads, preferred_element_type=jnp.float32
    ) * HEAD_DIM ** (-0.5)
    bin_index = first_bin + jnp.arange(key_count, dtype=jnp.int32)
    bin_float = bin_index.astype(jnp.float32)
    distance = jnp.abs(bin_float[None, :] - centres[:, None])
    usable = (
        (distance <= RADIUS) & (bin_index[None, :] >= 0) & (bin_index[None, :] < total_bins) & True
    )
    scores = jnp.where(usable[None], scores - slopes[:, None, None] * distance[None, :, :], -1e30)
    new_max = jnp.maximum(run_max, jnp.max(scores, axis=2))
    exps = jnp.exp(scores - jnp.maximum(new_max, -1e29)[:, :, None])
    factor = jnp.exp(run_max - new_max)
    new_sum = run_sum * factor + jnp.sum(exps, axis=2)
    gained = jnp.einsum(
        "gqk,kgd->qgd", exps.astype(jnp.bfloat16), value_heads, preferred_element_type=jnp.float32
    )
    new_out = run_out.reshape(row_count, groups, HEAD_DIM) * factor.T[:, :, None] + gained
    return (new_max, new_sum, new_out.reshape(row_count, groups * HEAD_DIM))


def local(queries, cell_types, promoters, offsets, cell_embed, bin_keys, bin_values, slopes, w_out):
    seq_count = lax.axis_size("seq")
    position = lax.axis_index("seq")
    bins_dev = bin_keys.shape[0]
    total_bins = bins_dev * seq_count
    row_count = queries.shape[0]
    groups = slopes.shape[0]
    one_hot = (
        cell_types[:, None] == jnp.arange(cell_embed.shape[0], dtype=jnp.int32)[None, :]
    ).astype(jnp.bfloat16)
    embedded = jnp.dot(one_hot, cell_embed, preferred_element_type=jnp.float32)
    query_rows = (queries.astype(jnp.float32) + embedded).astype(jnp.bfloat16)
    centres = (promoters + offsets).astype(jnp.float32)
    blank_state = (
        jnp.full((groups, row_count), -1e30, jnp.float32),
        jnp.zeros((groups, row_count), jnp.float32),
        jnp.zeros((row_count, queries.shape[1]), jnp.float32),
    )
    max_hops = min(HOPS, seq_count - 1)
    at_home = attend(
        blank_state,
        query_rows,
        centres,
        bin_keys,
        bin_values,
        position * bins_dev,
        slopes,
        total_bins,
    )
    carried = at_home
    for stride in range(1, max_hops + 1):
        for distance in (stride, -stride):
            near_keys, near_values = shifted((bin_keys, bin_values), "seq", distance)
            carried = attend(
                carried,
                query_rows,
                centres,
                near_keys,
                near_values,
                (position - distance) * bins_dev,
                slopes,
                total_bins,
            )
    run_max, run_sum, run_out = carried
    pooled = (
        (run_out.reshape(row_count, groups, HEAD_DIM) / run_sum.T[:, :, None])
        .reshape(row_count, groups * HEAD_DIM)
        .astype(jnp.bfloat16)
    )
    partial_sums = jnp.dot(pooled, w_out, preferred_element_type=jnp.float32)
    return lax.psum_scatter(
        partial_sums.astype(jnp.bfloat16), "head", scatter_dimension=1, tiled=True
    )


def solution(mesh):
    return jax.shard_map(
        local,
        mesh=mesh,
        in_specs=(
            P("seq", "head"),
            P("seq"),
            P("seq"),
            P("seq"),
            P(None, "head"),
            P("seq", "head"),
            P("seq", "head"),
            P("head"),
            P("head", None),
        ),
        out_specs=P("seq", "head"),
        check_vma=False,
    )
```

profile of v0, /device:TPU:2, one launch (start us, length us, event | category | flops | bytes accessed | tf_op | source)
XLA Modules:
  0.0 540.0 jit_solution(12206683307309627332)
XLA Ops:
  6.5 7.9 %collective-permute-start.6 = (bf16[2048,384]{1,0:T(8,128)(2,1)}, bf16[2048,384]{1,0:T(8,128)(2,1)}, u32[]{:S(2)}, u32[]{:S(2)}) collective-permute-start(bf16[2048,384]{1,0:T(8,128)(2,1)} %param.14), channel_id=1, source_target_pairs={{8,0},{12,4},{16,8},{20,12},{24,16},{28,20},{32,24},{36,28},{40,32... | collective-permute-start | bytes 4718600 | tf_op jit(solution)/shard_map/ppermute | solution.py:14
  18.3 7.0 %collective-permute-start.2 = (bf16[2048,384]{1,0:T(8,128)(2,1)}, bf16[2048,384]{1,0:T(8,128)(2,1)}, u32[]{:S(2)}, u32[]{:S(2)}) collective-permute-start(bf16[2048,384]{1,0:T(8,128)(2,1)} %param.14), channel_id=1, source_target_pairs={{4,0},{8,4},{12,8},{16,12},{20,16},{24,20},{28,24},{32,28},{36,32}... | collective-permute-start | bytes 4718600 | tf_op jit(solution)/shard_map/ppermute | solution.py:14
  28.6 2.7 copy.57
  35.0 3.6 subtract_abs_fusion.1
  40.4 61.7 %collective-permute-done.2 = bf16[2048,384]{1,0:T(8,128)(2,1)} collective-permute-done((bf16[2048,384]{1,0:T(8,128)(2,1)}, bf16[2048,384]{1,0:T(8,128)(2,1)}, u32[]{:S(2)}, u32[]{:S(2)}) %collective-permute-start.2) | collective-permute-done | bytes 1572896 | tf_op jit(solution)/shard_map/ppermute | solution.py:14
  102.1 17.6 %collective-permute-start.10 = (bf16[2048,384]{1,0:T(8,128)(2,1)}, bf16[2048,384]{1,0:T(8,128)(2,1)}, u32[]{:S(2)}, u32[]{:S(2)}) collective-permute-start(bf16[2048,384]{1,0:T(8,128)(2,1)} %param.14), channel_id=1, source_target_pairs={{12,0},{16,4},{20,8},{24,12},{28,16},{32,20},{36,24},{40,28},{44,3... | collective-permute-start | bytes 4718600 | tf_op jit(solution)/shard_map/ppermute | solution.py:14
  119.8 4.1 fusion.177
  131.1 5.2 fusion.175
  138.9 6.9 %collective-permute-start.14 = (bf16[2048,384]{1,0:T(8,128)(2,1)}, bf16[2048,384]{1,0:T(8,128)(2,1)}, u32[]{:S(2)}, u32[]{:S(2)}) collective-permute-start(bf16[2048,384]{1,0:T(8,128)(2,1)} %param.14), channel_id=1, source_target_pairs={{16,0},{20,4},{24,8},{28,12},{32,16},{36,20},{40,24},{44,28},{48,3... | collective-permute-start | bytes 4718600 | tf_op jit(solution)/shard_map/ppermute | solution.py:14
  153.1 37.0 %collective-permute-done = bf16[2048,384]{1,0:T(8,128)(2,1)} collective-permute-done((bf16[2048,384]{1,0:T(8,128)(2,1)}, bf16[2048,384]{1,0:T(8,128)(2,1)}, u32[]{:S(2)}, u32[]{:S(2)}) %collective-permute-start) | collective-permute-done | bytes 1572896 | tf_op jit(solution)/shard_map/ppermute | solution.py:14
  192.1 2.6 copy.59
  194.7 29.6 %collective-permute-done.10 = bf16[2048,384]{1,0:T(8,128)(2,1)} collective-permute-done((bf16[2048,384]{1,0:T(8,128)(2,1)}, bf16[2048,384]{1,0:T(8,128)(2,1)}, u32[]{:S(2)}, u32[]{:S(2)}) %collective-permute-start.10) | collective-permute-done | bytes 1572896 | tf_op jit(solution)/shard_map/ppermute | solution.py:14
  224.3 12.5 %collective-permute-start.7 = (bf16[2048,384]{1,0:T(8,128)(2,1)}, bf16[2048,384]{1,0:T(8,128)(2,1)}, u32[]{:S(2)}, u32[]{:S(2)}) collective-permute-start(bf16[2048,384]{1,0:T(8,128)(2,1)} %param.15), channel_id=1, source_target_pairs={{8,0},{12,4},{16,8},{20,12},{24,16},{28,20},{32,24},{36,28},{40,32... | collective-permute-start | bytes 4718600 | tf_op jit(solution)/shard_map/ppermute | solution.py:14
  239.5 5.4 fusion.176
  245.5 3.6 fusion.174
  249.1 4.2 fusion.178
  253.3 9.5 %collective-permute-start.11 = (bf16[2048,384]{1,0:T(8,128)(2,1)}, bf16[2048,384]{1,0:T(8,128)(2,1)}, u32[]{:S(2)}, u32[]{:S(2)}) collective-permute-start(bf16[2048,384]{1,0:T(8,128)(2,1)} %param.15), channel_id=1, source_target_pairs={{12,0},{16,4},{20,8},{24,12},{28,16},{32,20},{36,24},{40,28},{44,3... | collective-permute-start | bytes 4718600 | tf_op jit(solution)/shard_map/ppermute | solution.py:14
  266.9 5.2 fusion.179
  272.1 3.5 fusion.173
  275.7 3.5 fusion.180
  279.2 16.3 %collective-permute-start.13 = (bf16[2048,384]{1,0:T(8,128)(2,1)}, bf16[2048,384]{1,0:T(8,128)(2,1)}, u32[]{:S(2)}, u32[]{:S(2)}) collective-permute-start(bf16[2048,384]{1,0:T(8,128)(2,1)} %param.15), channel_id=1, source_target_pairs={{0,16},{4,20},{8,24},{12,28},{16,32},{20,36},{24,40},{28,44},{32,4... | collective-permute-start | bytes 4718600 | tf_op jit(solution)/shard_map/ppermute | solution.py:14
  298.1 3.3 fusion.181
  309.1 19.6 %collective-permute-start.15 = (bf16[2048,384]{1,0:T(8,128)(2,1)}, bf16[2048,384]{1,0:T(8,128)(2,1)}, u32[]{:S(2)}, u32[]{:S(2)}) collective-permute-start(bf16[2048,384]{1,0:T(8,128)(2,1)} %param.15), channel_id=1, source_target_pairs={{16,0},{20,4},{24,8},{28,12},{32,16},{36,20},{40,24},{44,28},{48,3... | collective-permute-start | bytes 4718600 | tf_op jit(solution)/shard_map/ppermute | solution.py:14
  331.3 34.2 %collective-permute-start.3 = (bf16[2048,384]{1,0:T(8,128)(2,1)}, bf16[2048,384]{1,0:T(8,128)(2,1)}, u32[]{:S(2)}, u32[]{:S(2)}) collective-permute-start(bf16[2048,384]{1,0:T(8,128)(2,1)} %param.15), channel_id=1, source_target_pairs={{4,0},{8,4},{12,8},{16,12},{20,16},{24,20},{28,24},{32,28},{36,32}... | collective-permute-start | bytes 4718600 | tf_op jit(solution)/shard_map/ppermute | solution.py:14
  368.1 32.9 %collective-permute-start.1 = (bf16[2048,384]{1,0:T(8,128)(2,1)}, bf16[2048,384]{1,0:T(8,128)(2,1)}, u32[]{:S(2)}, u32[]{:S(2)}) collective-permute-start(bf16[2048,384]{1,0:T(8,128)(2,1)} %param.15), channel_id=1, source_target_pairs={{0,4},{4,8},{8,12},{12,16},{16,20},{20,24},{24,28},{28,32},{32,36}... | collective-permute-start | bytes 4718600 | tf_op jit(solution)/shard_map/ppermute | solution.py:14
  403.7 3.6 fusion.8
  416.3 3.7 fusion.69
  427.0 12.8 %collective-permute-done.15 = bf16[2048,384]{1,0:T(8,128)(2,1)} collective-permute-done((bf16[2048,384]{1,0:T(8,128)(2,1)}, bf16[2048,384]{1,0:T(8,128)(2,1)}, u32[]{:S(2)}, u32[]{:S(2)}) %collective-permute-start.15) | collective-permute-done | bytes 1572896 | tf_op jit(solution)/shard_map/ppermute | solution.py:14
  442.5 29.9 %collective-permute-done.3 = bf16[2048,384]{1,0:T(8,128)(2,1)} collective-permute-done((bf16[2048,384]{1,0:T(8,128)(2,1)}, bf16[2048,384]{1,0:T(8,128)(2,1)}, u32[]{:S(2)}, u32[]{:S(2)}) %collective-permute-start.3) | collective-permute-done | bytes 1572896 | tf_op jit(solution)/shard_map/ppermute | solution.py:14
  475.0 4.4 fusion.81
  487.1 3.5 fusion.127
  492.0 39.1 %reduce-scatter.4.cloned.1.call-done = bf16[384,128]{1,0:T(8,128)(2,1)} async-done(((bf16[1536,128]{1,0:T(8,128)(2,1)}), bf16[384,128]{1,0:T(8,128)(2,1)}) %reduce-scatter.4.cloned.1.call-update) | async-done | bytes 98320
  (259 shorter events, 88.5 us)
Async XLA Ops:
  6.5 484.1 %copy-start = (bf16[384,1536]{1,0:T(8,128)(2,1)S(1)}, bf16[384,1536]{1,0:T(8,128)(2,1)}, u32[]{:S(2)}) copy-start(bf16[384,1536]{1,0:T(8,128)(2,1)} %param.17) | copy-start | bytes 3538948
  6.5 524.6 %reduce-scatter.4.cloned.1.call-start = ((), (), s32[]{:S(2)}) async-start(), calls=%async_computation.1 | async-start | bytes 491520
  6.5 122.6 %collective-permute-start.6 = (bf16[2048,384]{1,0:T(8,128)(2,1)}, bf16[2048,384]{1,0:T(8,128)(2,1)}, u32[]{:S(2)}, u32[]{:S(2)}) collective-permute-start(bf16[2048,384]{1,0:T(8,128)(2,1)} %param.14), channel_id=1, source_target_pairs={{8,0},{12,4},{16,8},{20,12},{24,16},{28,20},{32,24},{36,28},{40,32... | collective-permute-start | bytes 4718600 | tf_op jit(solution)/shard_map/ppermute | solution.py:14
  14.4 124.5 %collective-permute-start.4 = (bf16[2048,384]{1,0:T(8,128)(2,1)}, bf16[2048,384]{1,0:T(8,128)(2,1)}, u32[]{:S(2)}, u32[]{:S(2)}) collective-permute-start(bf16[2048,384]{1,0:T(8,128)(2,1)} %param.14), channel_id=1, source_target_pairs={{0,8},{4,12},{8,16},{12,20},{16,24},{20,28},{24,32},{28,36},{32,40... | collective-permute-start | bytes 4718600 | tf_op jit(solution)/shard_map/ppermute | solution.py:14
  16.4 132.1 %collective-permute-start.8 = (bf16[2048,384]{1,0:T(8,128)(2,1)}, bf16[2048,384]{1,0:T(8,128)(2,1)}, u32[]{:S(2)}, u32[]{:S(2)}) collective-permute-start(bf16[2048,384]{1,0:T(8,128)(2,1)} %param.14), channel_id=1, source_target_pairs={{0,12},{4,16},{8,20},{12,24},{16,28},{20,32},{24,36},{28,40},{32,4... | collective-permute-start | bytes 4718600 | tf_op jit(solution)/shard_map/ppermute | solution.py:14
  18.3 83.8 %collective-permute-start.2 = (bf16[2048,384]{1,0:T(8,128)(2,1)}, bf16[2048,384]{1,0:T(8,128)(2,1)}, u32[]{:S(2)}, u32[]{:S(2)}) collective-permute-start(bf16[2048,384]{1,0:T(8,128)(2,1)} %param.14), channel_id=1, source_target_pairs={{4,0},{8,4},{12,8},{16,12},{20,16},{24,20},{28,24},{32,28},{36,32}... | collective-permute-start | bytes 4718600 | tf_op jit(solution)/shard_map/ppermute | solution.py:14
  25.3 164.8 %collective-permute-start = (bf16[2048,384]{1,0:T(8,128)(2,1)}, bf16[2048,384]{1,0:T(8,128)(2,1)}, u32[]{:S(2)}, u32[]{:S(2)}) collective-permute-start(bf16[2048,384]{1,0:T(8,128)(2,1)} %param.14), channel_id=1, source_target_pairs={{0,4},{4,8},{8,12},{12,16},{16,20},{20,24},{24,28},{28,32},{32,36}... | collective-permute-start | bytes 4718600 | tf_op jit(solution)/shard_map/ppermute | solution.py:14
  33.2 86.6 %copy-start.30 = (bf16[128,384]{0,1:T(8,128)(2,1)}, bf16[128,384]{0,1:T(8,128)(2,1)S(1)}, u32[]{:S(2)}) copy-start(bf16[128,384]{0,1:T(8,128)(2,1)S(1)} %copy.56) | copy-start | bytes 294916
  35.0 84.8 %copy-start.19 = (bf16[2048,384]{0,1:T(8,128)(2,1)S(1)}, bf16[2048,384]{0,1:T(8,128)(2,1)}, u32[]{:S(2)}) copy-start(bf16[2048,384]{0,1:T(8,128)(2,1)} %copy.57) | copy-start | bytes 4718596
  35.0 84.8 %copy-start.86 = (f32[4]{0:T(128)S(1)}, f32[4]{0:T(128)}, u32[]{:S(2)}) copy-start(f32[4]{0:T(128)} %param.16) | copy-start | bytes 52
  38.6 85.3 %copy-start.67 = (pred[2048]{0:T(1024)(128)(4,1)S(1)}, pred[2048]{0:T(1024)(128)(4,1)}, u32[]{:S(2)}) copy-start(pred[2048]{0:T(1024)(128)(4,1)} %get-tuple-element.71) | copy-start | bytes 6148
  38.6 85.3 %copy-start.68 = (pred[2048]{0:T(1024)(128)(4,1)S(1)}, pred[2048]{0:T(1024)(128)(4,1)}, u32[]{:S(2)}) copy-start(pred[2048]{0:T(1024)(128)(4,1)} %get-tuple-element.72) | copy-start | bytes 6148
  38.6 85.3 %copy-start.69 = (pred[2048]{0:T(1024)(128)(4,1)S(1)}, pred[2048]{0:T(1024)(128)(4,1)}, u32[]{:S(2)}) copy-start(pred[2048]{0:T(1024)(128)(4,1)} %get-tuple-element.73) | copy-start | bytes 6148
  38.6 85.3 %copy-start.70 = (pred[2048]{0:T(1024)(128)(4,1)S(1)}, pred[2048]{0:T(1024)(128)(4,1)}, u32[]{:S(2)}) copy-start(pred[2048]{0:T(1024)(128)(4,1)} %get-tuple-element.74) | copy-start | bytes 6148
  38.6 85.3 %copy-start.71 = (pred[2048]{0:T(1024)(128)(4,1)S(1)}, pred[2048]{0:T(1024)(128)(4,1)}, u32[]{:S(2)}) copy-start(pred[2048]{0:T(1024)(128)(4,1)} %get-tuple-element.65) | copy-start | bytes 6148
  38.6 85.3 %copy-start.72 = (pred[2048]{0:T(1024)(128)(4,1)S(1)}, pred[2048]{0:T(1024)(128)(4,1)}, u32[]{:S(2)}) copy-start(pred[2048]{0:T(1024)(128)(4,1)} %get-tuple-element.66) | copy-start | bytes 6148
  38.6 85.3 %copy-start.35 = (f32[2048]{0:T(1024)S(1)}, f32[2048]{0:T(1024)}, u32[]{:S(2)}) copy-start(f32[2048]{0:T(1024)} %copy-done.34) | copy-start | bytes 24580
  38.6 85.3 %copy-start.37 = (f32[2048]{0:T(1024)S(1)}, f32[2048]{0:T(1024)}, u32[]{:S(2)}) copy-start(f32[2048]{0:T(1024)} %copy-done.36) | copy-start | bytes 24580
  102.1 122.2 %collective-permute-start.10 = (bf16[2048,384]{1,0:T(8,128)(2,1)}, bf16[2048,384]{1,0:T(8,128)(2,1)}, u32[]{:S(2)}, u32[]{:S(2)}) collective-permute-start(bf16[2048,384]{1,0:T(8,128)(2,1)} %param.14), channel_id=1, source_target_pairs={{12,0},{16,4},{20,8},{24,12},{28,16},{32,20},{36,24},{40,28},{44,3... | collective-permute-start | bytes 4718600 | tf_op jit(solution)/shard_map/ppermute | solution.py:14
  129.1 124.2 %collective-permute-start.12 = (bf16[2048,384]{1,0:T(8,128)(2,1)}, bf16[2048,384]{1,0:T(8,128)(2,1)}, u32[]{:S(2)}, u32[]{:S(2)}) collective-permute-start(bf16[2048,384]{1,0:T(8,128)(2,1)} %param.14), channel_id=1, source_target_pairs={{0,16},{4,20},{8,24},{12,28},{16,32},{20,36},{24,40},{28,44},{32,4... | collective-permute-start | bytes 4718600 | tf_op jit(solution)/shard_map/ppermute | solution.py:14
  136.3 108.6 %copy-start.45 = (f32[4,128]{1,0:T(4,128)}, f32[4,128]{1,0:T(4,128)S(1)}, u32[]{:S(2)}) copy-start(f32[4,128]{1,0:T(4,128)S(1)} %get-tuple-element.51) | copy-start | bytes 6148
  138.9 140.3 %collective-permute-start.14 = (bf16[2048,384]{1,0:T(8,128)(2,1)}, bf16[2048,384]{1,0:T(8,128)(2,1)}, u32[]{:S(2)}, u32[]{:S(2)}) collective-permute-start(bf16[2048,384]{1,0:T(8,128)(2,1)} %param.14), channel_id=1, source_target_pairs={{16,0},{20,4},{24,8},{28,12},{32,16},{36,20},{40,24},{44,28},{48,3... | collective-permute-start | bytes 4718600 | tf_op jit(solution)/shard_map/ppermute | solution.py:14
  148.4 91.0 %copy-start.87 = (f32[4]{0:T(128)S(1)}, f32[4]{0:T(128)}, u32[]{:S(2)}) copy-start(f32[4]{0:T(128)} %param.16) | copy-start | bytes 52
  148.4 160.7 %collective-permute-start.9 = (bf16[2048,384]{1,0:T(8,128)(2,1)}, bf16[2048,384]{1,0:T(8,128)(2,1)}, u32[]{:S(2)}, u32[]{:S(2)}) collective-permute-start(bf16[2048,384]{1,0:T(8,128)(2,1)} %param.15), channel_id=1, source_target_pairs={{0,12},{4,16},{8,20},{12,24},{16,28},{20,32},{24,36},{28,40},{32,4... | collective-permute-start | bytes 4718600 | tf_op jit(solution)/shard_map/ppermute | solution.py:14
  190.2 141.1 %collective-permute-start.5 = (bf16[2048,384]{1,0:T(8,128)(2,1)}, bf16[2048,384]{1,0:T(8,128)(2,1)}, u32[]{:S(2)}, u32[]{:S(2)}) collective-permute-start(bf16[2048,384]{1,0:T(8,128)(2,1)} %param.15), channel_id=1, source_target_pairs={{0,8},{4,12},{8,16},{12,20},{16,24},{20,28},{24,32},{28,36},{32,40... | collective-permute-start | bytes 4718600 | tf_op jit(solution)/shard_map/ppermute | solution.py:14
  224.3 143.8 %collective-permute-start.7 = (bf16[2048,384]{1,0:T(8,128)(2,1)}, bf16[2048,384]{1,0:T(8,128)(2,1)}, u32[]{:S(2)}, u32[]{:S(2)}) collective-permute-start(bf16[2048,384]{1,0:T(8,128)(2,1)} %param.15), channel_id=1, source_target_pairs={{8,0},{12,4},{16,8},{20,12},{24,16},{28,20},{32,24},{36,28},{40,32... | collective-permute-start | bytes 4718600 | tf_op jit(solution)/shard_map/ppermute | solution.py:14
  253.3 160.2 %collective-permute-start.11 = (bf16[2048,384]{1,0:T(8,128)(2,1)}, bf16[2048,384]{1,0:T(8,128)(2,1)}, u32[]{:S(2)}, u32[]{:S(2)}) collective-permute-start(bf16[2048,384]{1,0:T(8,128)(2,1)} %param.15), channel_id=1, source_target_pairs={{12,0},{16,4},{20,8},{24,12},{28,16},{32,20},{36,24},{40,28},{44,3... | collective-permute-start | bytes 4718600 | tf_op jit(solution)/shard_map/ppermute | solution.py:14
  279.2 145.2 %collective-permute-start.13 = (bf16[2048,384]{1,0:T(8,128)(2,1)}, bf16[2048,384]{1,0:T(8,128)(2,1)}, u32[]{:S(2)}, u32[]{:S(2)}) collective-permute-start(bf16[2048,384]{1,0:T(8,128)(2,1)} %param.15), channel_id=1, source_target_pairs={{0,16},{4,20},{8,24},{12,28},{16,32},{20,36},{24,40},{28,44},{32,4... | collective-permute-start | bytes 4718600 | tf_op jit(solution)/shard_map/ppermute | solution.py:14
  309.1 94.6 %copy-start.38 = (f32[4,128]{1,0:T(4,128)S(1)}, f32[4,128]{1,0:T(4,128)}, u32[]{:S(2)}) copy-start(f32[4,128]{1,0:T(4,128)} %get-tuple-element.17) | copy-start | bytes 6148
  309.1 130.8 %collective-permute-start.15 = (bf16[2048,384]{1,0:T(8,128)(2,1)}, bf16[2048,384]{1,0:T(8,128)(2,1)}, u32[]{:S(2)}, u32[]{:S(2)}) collective-permute-start(bf16[2048,384]{1,0:T(8,128)(2,1)} %param.15), channel_id=1, source_target_pairs={{16,0},{20,4},{24,8},{28,12},{32,16},{36,20},{40,24},{44,28},{48,3... | collective-permute-start | bytes 4718600 | tf_op jit(solution)/shard_map/ppermute | solution.py:14
  331.3 141.0 %collective-permute-start.3 = (bf16[2048,384]{1,0:T(8,128)(2,1)}, bf16[2048,384]{1,0:T(8,128)(2,1)}, u32[]{:S(2)}, u32[]{:S(2)}) collective-permute-start(bf16[2048,384]{1,0:T(8,128)(2,1)} %param.15), channel_id=1, source_target_pairs={{4,0},{8,4},{12,8},{16,12},{20,16},{24,20},{28,24},{32,28},{36,32}... | collective-permute-start | bytes 4718600 | tf_op jit(solution)/shard_map/ppermute | solution.py:14
  368.1 117.3 %collective-permute-start.1 = (bf16[2048,384]{1,0:T(8,128)(2,1)}, bf16[2048,384]{1,0:T(8,128)(2,1)}, u32[]{:S(2)}, u32[]{:S(2)}) collective-permute-start(bf16[2048,384]{1,0:T(8,128)(2,1)} %param.15), channel_id=1, source_target_pairs={{0,4},{4,8},{8,12},{12,16},{16,20},{20,24},{24,28},{28,32},{32,36}... | collective-permute-start | bytes 4718600 | tf_op jit(solution)/shard_map/ppermute | solution.py:14
  (76 other events, 472.3 us)
Sparse Core Ops, SparseCore 0:
  492.2 38.9 reduce-scatter.3
where the time goes:
time: 549 us; the launch traced here: 540 us
  waiting for transfers between devices  210 us (38%)
  starting transfers between devices  176 us (32%)
  matrix products  60.1 us (11%)
  local copies, waits for them, and re-layouts  52.5 us (10%)
  other arithmetic  26.2 us (5%)
  between operations  14.9 us (3%)
    ppermute x16, starting transfers between devices, shifted(): lax.ppermute(value, axis, [(source, source + steps) for source in range(l...  176 us
    ppermute x16, waiting for transfers between devices, shifted(): lax.ppermute(value, axis, [(source, source + steps) for source in range(l...  171 us
    ppermute x16, local copies, waits for them, and re-layouts, shifted(): lax.ppermute(value, axis, [(source, source + steps) for source in range(l...  40.9 us
    unnamed x2, waiting for transfers between devices  39.1 us
    dot_general x9, matrix products, attend(): jnp.einsum('qgd,kgd->gqk', query_heads, key_heads, preferred_element_type...  37.9 us
    dot_general x9, matrix products, attend(): jnp.einsum('gqk,kgd->qgd', exps.astype(jnp.bfloat16), value_heads, prefer...  20.6 us
    reduce_sum x9, other arithmetic, attend(): new_sum = run_sum * factor + jnp.sum(exps, axis=2)  13.8 us
    unnamed x186, local copies, waits for them, and re-layouts  11.5 us
  transfers between devices with their start and end apart: 17, of which 6 were waited for; matrix products, arithmetic and copies ran while one was open for 23% of the time, Pallas kernels for 0%

commit v1 on v0

v1 whole, which is shorter than its diff:
```python
import functools
import math

import jax
import jax.numpy as jnp
from jax import lax
from jax.experimental import pallas as pl
from jax.experimental.pallas import tpu as pltpu
from jax.sharding import PartitionSpec as P

HEAD_DIM = 96
RADIUS = 7812
SHIFT = 64
HOPS = 4
LANES = 128
LOG2E = math.log2(math.e)
SCALE2 = LOG2E / math.sqrt(HEAD_DIM)
EMPTY = -16384.0
SUM_LO, SUM_HI = 2.0**-60, 2.0**100
TILE = 512


def column(row):
    n = row.shape[1]
    eye = lax.broadcasted_iota(jnp.int32, (n, n), 0) == lax.broadcasted_iota(jnp.int32, (n, n), 1)
    return jnp.sum(jnp.where(eye, row, 0.0), axis=1, keepdims=True)


def query_kernel(groups, types_ref, promoters_ref, offsets_ref, base_ref, queries_ref, embed_ref, out_ref):
    rows = queries_ref.shape[0]
    kinds = embed_ref.shape[0]
    one_hot = (lax.broadcasted_iota(jnp.int32, (kinds, rows), 0) == types_ref[...]).astype(jnp.float32)
    embedded = lax.dot_general(
        one_hot.T.astype(jnp.bfloat16), embed_ref[...], (((1,), (0,)), ((), ())), preferred_element_type=jnp.float32
    )
    query = (queries_ref[...].astype(jnp.float32) + embedded).astype(jnp.bfloat16)
    place = promoters_ref[...] + offsets_ref[...] - base_ref[0] + SHIFT
    coarse = lax.shift_right_arithmetic(place, 4)
    fine = place - coarse * 16
    coarse = column((coarse * 16).astype(jnp.float32))
    fine = column(fine.astype(jnp.float32))
    lane = lax.broadcasted_iota(jnp.int32, (rows, LANES - HEAD_DIM), 1)
    extra = jnp.where(lane == 0, coarse, jnp.where(lane == 1, fine, 0.0)).astype(jnp.bfloat16)
    for g in range(groups):
        out_ref[:, g * LANES : g * LANES + HEAD_DIM] = query[:, g * HEAD_DIM : (g + 1) * HEAD_DIM]
        out_ref[:, g * LANES + HEAD_DIM : (g + 1) * LANES] = extra


def bins_kernel(groups, keys_ref, values_ref, keys_out, values_out):
    count = keys_ref.shape[0]
    lane = lax.broadcasted_iota(jnp.int32, (count, LANES - HEAD_DIM), 1)
    blank = jnp.zeros((count, LANES - HEAD_DIM), jnp.bfloat16)
    ones = jnp.where(lane == 0, 1.0, 0.0).astype(jnp.bfloat16)
    for g in range(groups):
        keys_out[g, :, :HEAD_DIM] = keys_ref[:, g * HEAD_DIM : (g + 1) * HEAD_DIM]
        keys_out[g, :, HEAD_DIM:] = blank
        values_out[g, :, :HEAD_DIM] = values_ref[:, g * HEAD_DIM : (g + 1) * HEAD_DIM]
        values_out[g, :, HEAD_DIM:] = ones


def unit_kernel(strides, bins, slopes_ref, ok_ref, *refs):
    n = len(strides)
    query_refs, (keys_ref, values_ref), out_refs, (acc_ref, bad_ref) = refs[:n], refs[n : n + 2], refs[n + 2 : 2 * n + 2], refs[2 * n + 2 :]
    g = pl.program_id(0)
    rows = query_refs[0].shape[0]
    slope = slopes_ref[g] * LOG2E

    def centre_of(i):
        extra = query_refs[i][:, HEAD_DIM:LANES].astype(jnp.float32)
        place = extra[:, 0:1] + extra[:, 1:2] - SHIFT
        return place - float(bins * strides[i]), None

    @pl.when(g == 0)
    def _():
        for i in range(n):
            extra = query_refs[i][:, HEAD_DIM:LANES].astype(jnp.float32)
            place = extra[:, 0:1] + extra[:, 1:2] - float(SHIFT + bins * strides[i])
            bad_ref[i] = jnp.broadcast_to(place, (rows, LANES))

    def prepared(i):
        centre = bad_ref[i][:, 0:1]
        nearest = jnp.maximum(0.0, jnp.maximum(-centre, centre - float(bins - 1)))
        alive = (nearest <= RADIUS) & (ok_ref[i] > 0)
        return centre, nearest, alive

    def arguments(i, centre, nearest, start, size):
        stride = strides[i]
        query = query_refs[i][:, pl.ds(pl.multiple_of(g * LANES, LANES), LANES)]
        keys = keys_ref[0, pl.ds(start, size), :]
        raw = lax.dot_general(query, keys, (((1,), (1,)), ((), ())), preferred_element_type=jnp.float32)
        position = (start + lax.broadcasted_iota(jnp.int32, (1, size), 1)).astype(jnp.float32)
        if stride >= 2:
            bias = -slope * position
        elif stride <= -2:
            bias = -slope * (float(bins - 1) - position)
        else:
            bias = -slope * (jnp.abs(position - centre) - nearest)
        usable = None
        if stride >= 3:
            usable = position <= centre + float(RADIUS)
        elif stride <= -3:
            usable = position >= centre - float(RADIUS)
        return raw * SCALE2 + bias, usable

    def finish(i, acc, shift, nearest, alive):
        lane = lax.broadcasted_iota(jnp.int32, (rows, LANES), 1)
        exponent = shift - slope * nearest
        coarse = jnp.where(alive, jnp.round(exponent * 0.0625) * 16.0, EMPTY)
        factor = jnp.where(alive, jnp.exp2(exponent - coarse), 0.0)
        scaled = jnp.where(alive, acc * factor, 0.0)
        total = scaled[:, HEAD_DIM : HEAD_DIM + 1]
        high = total.astype(jnp.bfloat16).astype(jnp.float32)
        scaled = jnp.where(lane == HEAD_DIM + 1, total - high, scaled)
        scaled = jnp.where(lane == HEAD_DIM + 2, coarse, scaled)
        return scaled.astype(jnp.bfloat16)

    wrong = jnp.zeros((rows, 1), jnp.float32)
    for i in range(n):
        centre, nearest, alive = prepared(i)
        acc = jnp.zeros((rows, LANES), jnp.float32)
        for start in range(0, bins, TILE):
            logs, usable = arguments(i, centre, nearest, start, TILE)
            weights = jnp.exp2(logs)
            if usable is not None:
                weights = jnp.where(usable, weights, 0.0)
            acc += jnp.dot(weights.astype(jnp.bfloat16), values_ref[0, start : start + TILE, :], preferred_element_type=jnp.float32)
        total = acc[:, HEAD_DIM : HEAD_DIM + 1]
        fine = (total >= SUM_LO) & (total <= SUM_HI)
        wrong = jnp.maximum(wrong, jnp.where(alive & jnp.logical_not(fine), 1.0, 0.0))
        out_refs[i][...] = finish(i, acc, jnp.zeros((rows, 1), jnp.float32), nearest, alive)

    @pl.when(jnp.max(wrong) > 0.0)
    def _():
        for i in range(n):
            centre, nearest, alive = prepared(i)

            def largest(k, so_far):
                logs, usable = arguments(i, centre, nearest, pl.multiple_of(k * LANES, LANES), LANES)
                if usable is not None:
                    logs = jnp.where(usable, logs, -1e30)
                return jnp.maximum(so_far, jnp.max(logs, axis=1, keepdims=True))

            shift = lax.fori_loop(0, bins // LANES, largest, jnp.full((rows, 1), -1e30, jnp.float32))
            acc_ref[...] = jnp.zeros_like(acc_ref)

            @pl.loop(0, bins // LANES)
            def _(k):
                start = pl.multiple_of(k * LANES, LANES)
                logs, usable = arguments(i, centre, nearest, start, LANES)
                weights = jnp.exp2(logs - shift)
                if usable is not None:
                    weights = jnp.where(usable, weights, 0.0)
                acc_ref[...] += jnp.dot(
                    weights.astype(jnp.bfloat16), values_ref[0, pl.ds(start, LANES), :], preferred_element_type=jnp.float32
                )

            out_refs[i][...] = finish(i, acc_ref[...], shift, nearest, alive)


def merge_kernel(groups, place_ref, *refs):
    part_refs, (w_ref, keep_ref, send_ref) = refs[:-3], refs[-3:]
    rows = part_refs[0].shape[0]
    pooled = []
    for g in range(groups):
        parts = [ref[:, g * LANES : (g + 1) * LANES].astype(jnp.float32) for ref in part_refs]
        scales = [part[:, HEAD_DIM + 2 : HEAD_DIM + 3] for part in parts]
        top = functools.reduce(jnp.maximum, scales)
        acc = sum(part * jnp.exp2(scale - top) for part, scale in zip(parts, scales))
        total = acc[:, HEAD_DIM : HEAD_DIM + 1] + acc[:, HEAD_DIM + 1 : HEAD_DIM + 2]
        pooled.append((acc[:, :HEAD_DIM] / total).astype(jnp.bfloat16))
    width = w_ref.shape[1] // 4
    core, high = place_ref[0] & 1, place_ref[0] >> 1
    for k in range(2):
        row = jnp.where(k == 0, high, 1 - high) * 2
        for ref, lane in ((send_ref, 1 - core), (keep_ref, core)):
            start = pl.multiple_of((row + lane) * width, LANES)
            acc = jnp.zeros((rows, width), jnp.float32)
            for g in range(groups):
                weights = w_ref[g * HEAD_DIM : (g + 1) * HEAD_DIM, pl.ds(start, width)]
                acc += jnp.dot(pooled[g], weights, preferred_element_type=jnp.float32)
            ref[k] = acc.astype(ref.dtype)


SMEM = pl.BlockSpec(memory_space=pltpu.SMEM)


def attend(strides, slopes, ok, queries, keys, values):
    groups, bins, _ = keys.shape
    rows, width = queries[0].shape
    n = len(strides)
    return pl.pallas_call(
        functools.partial(unit_kernel, strides, bins),
        grid=(groups,),
        in_specs=[SMEM, SMEM]
        + [pl.BlockSpec((rows, width), lambda g: (0, 0))] * n
        + [pl.BlockSpec((1, bins, LANES), lambda g: (g, 0, 0))] * 2,
        out_specs=[pl.BlockSpec((rows, LANES), lambda g: (0, g))] * n,
        out_shape=[jax.ShapeDtypeStruct((rows, width), jnp.bfloat16)] * n,
        scratch_shapes=[pltpu.VMEM((rows, LANES), jnp.float32), pltpu.VMEM((n, rows, LANES), jnp.float32)],
        compiler_params=pltpu.CompilerParams(vmem_limit_bytes=28 * 2**20),
        cost_estimate=pl.CostEstimate(
            flops=4 * n * rows * bins * width, bytes_accessed=4 * bins * width, transcendentals=n * rows * bins * groups
        ),
        name="attend",
    )(slopes, ok, *queries, keys, values)


def prepare_queries(queries, cell_types, promoters, offsets, cell_embed, base, groups):
    rows = queries.shape[0]
    return pl.pallas_call(
        functools.partial(query_kernel, groups),
        in_specs=[pl.BlockSpec()] * 3 + [SMEM] + [pl.BlockSpec()] * 2,
        out_shape=jax.ShapeDtypeStruct((rows, groups * LANES), jnp.bfloat16),
        compiler_params=pltpu.CompilerParams(vmem_limit_bytes=8 * 2**20),
        name="prepare_queries",
    )(cell_types[None, :], promoters[None, :], offsets[None, :], base[None], queries, cell_embed)


def prepare_bins(keys, values, groups):
    bins = keys.shape[0]
    step = 512
    flat = pl.BlockSpec((step, keys.shape[1]), lambda i: (i, 0))
    split = pl.BlockSpec((groups, step, LANES), lambda i: (0, i, 0))
    return pl.pallas_call(
        functools.partial(bins_kernel, groups),
        grid=(bins // step,),
        in_specs=[flat, flat],
        out_specs=[split, split],
        out_shape=[jax.ShapeDtypeStruct((groups, bins, LANES), jnp.bfloat16)] * 2,
        compiler_params=pltpu.CompilerParams(vmem_limit_bytes=16 * 2**20),
        cost_estimate=pl.CostEstimate(flops=0, bytes_accessed=14 * 2**20, transcendentals=0),
        name="prepare_bins",
    )(keys, values)


def merge(place, parts, w_out, groups):
    rows = parts[0].shape[0]
    width = w_out.shape[1] // 4
    return pl.pallas_call(
        functools.partial(merge_kernel, groups),
        in_specs=[SMEM] + [pl.BlockSpec()] * (len(parts) + 1),
        out_shape=[
            jax.ShapeDtypeStruct((2, rows, width), jnp.float32),
            jax.ShapeDtypeStruct((2, rows, width), jnp.bfloat16),
        ],
        compiler_params=pltpu.CompilerParams(vmem_limit_bytes=16 * 2**20),
        name="merge",
    )(place[None], *parts, w_out)


def pairings(stride, count):
    ring = math.gcd(stride, count)
    length = count // ring
    even, odd = [], []
    for first in range(ring):
        order = [(first + stride * k) % count for k in range(length)]
        for k in range(0, length, 2):
            for table, a, b in ((even, order[k], order[k + 1]), (odd, order[k + 1], order[(k + 2) % length])):
                table += [(a, b), (b, a)]
    return even, odd


def rotated(value, steps):
    count = lax.axis_size("seq")
    return lax.ppermute(value, "seq", [(i, (i + steps) % count) for i in range(count)])


def local(queries, cell_types, promoters, offsets, cell_embed, bin_keys, bin_values, slopes, w_out):
    seq_count = lax.axis_size("seq")
    position = lax.axis_index("seq")
    place = lax.axis_index("head")
    bins = bin_keys.shape[0]
    groups = slopes.shape[0]
    mine = prepare_queries(queries, cell_types, promoters, offsets, cell_embed, position * bins, groups)
    strides = [1, 2, 3, 4]
    arrived = [(rotated(mine, d), rotated(mine, -d)) for d in strides]
    keys, values = prepare_bins(bin_keys, bin_values, groups)
    parts = list(attend((0,), slopes, jnp.ones((1,), jnp.int32), (mine,), keys, values))
    for d, pair in zip(strides, arrived):
        ok = jnp.stack([position >= d, position < seq_count - d]).astype(jnp.int32)
        up, down = attend((d, -d), slopes, ok, pair, keys, values)
        parts += [rotated(up, -d), rotated(down, d)]
    keep, send = merge(place, parts, w_out, groups)
    got = lax.ppermute(send, "head", [(i, i ^ 1) for i in range(4)])
    other = (keep[1] + got[1].astype(jnp.float32)).astype(jnp.bfloat16)
    last = lax.ppermute(other, "head", [(i, i ^ 2) for i in range(4)])
    return (keep[0] + got[0].astype(jnp.float32) + last.astype(jnp.float32)).astype(jnp.bfloat16)


def solution(mesh):
    return jax.shard_map(
        local,
        mesh=mesh,
        in_specs=(
            P("seq", "head"),
            P("seq"),
            P("seq"),
            P("seq"),
            P(None, "head"),
            P("seq", "head"),
            P("seq", "head"),
            P("head"),
            P("head", None),
        ),
        out_specs=P("seq", "head"),
        check_vma=False,
    )
```

time: 549 us -> 227 us (0.41)
  waiting for transfers between devices: 210 us -> 7.67 us
  Pallas kernels: 0 us -> 146 us
  starting transfers between devices: 176 us -> 60.3 us
  matrix products: 60.1 us -> 0 us
  local copies, waits for them, and re-layouts: 52.5 us -> 8.16 us
  other arithmetic: 26.2 us -> 0.99 us
  between operations: 14.9 us -> 0.18 us
    ppermute x16 -> x18, waiting for transfers between devices: 171 us -> 7.67 us  [the longest x1 6.56 us: local(): last = lax.ppermute(other, 'head', [(i, i ^ 2) for i in range(4)])]
    pallas_call x0 -> x8, Pallas kernels: none -> 146 us  [the longest x5 141 us: attend(): pl.pallas_call(functools.partial(unit_kernel, strides, bins), grid=(group...]
    ppermute x16 -> x18, starting transfers between devices: 176 us -> 60.3 us  [the longest x16 47 us: rotated(): lax.ppermute(value, 'seq', [(i, (i + steps) % count) for i in range(count)])]
    dot_general x20 -> x0, matrix products: 60.1 us -> none  [the longest x9 37.9 us: attend(): jnp.einsum('qgd,kgd->gqk', query_heads, key_heads, preferred_element_type...]
    ppermute x16 -> x0, local copies, waits for them, and re-layouts: 40.9 us -> none  [shifted(): lax.ppermute(value, axis, [(source, source + steps) for source in range(l...]
    unnamed x2 -> x0, waiting for transfers between devices: 39.1 us -> none
    reduce_sum x9 -> x0, other arithmetic: 13.8 us -> none  [attend(): new_sum = run_sum * factor + jnp.sum(exps, axis=2)]
    unnamed x186 -> x22, local copies, waits for them, and re-layouts: 11.5 us -> 8.16 us
  transfers between devices with their start and end apart: 17 -> 18, of which waited for: 6 -> 2; matrix products, arithmetic and copies ran while one was open for 23% -> 0% of each run, Pallas kernels for 0% -> 64%
where the time goes in v1:
time: 227 us; the launch traced here: 223 us
  Pallas kernels  146 us (64%)
  starting transfers between devices  60.3 us (27%)
  local copies, waits for them, and re-layouts  8.16 us (4%)
  waiting for transfers between devices  7.67 us (3%)
    pallas_call x5, Pallas kernels, attend(): pl.pallas_call(functools.partial(unit_kernel, strides, bins), grid=(group...  141 us
    ppermute x16, starting transfers between devices, rotated(): lax.ppermute(value, 'seq', [(i, (i + steps) % count) for i in range(count)])  47 us
    ppermute x1, starting transfers between devices, local(): got = lax.ppermute(send, 'head', [(i, i ^ 1) for i in range(4)])  13.3 us
    unnamed x22, local copies, waits for them, and re-layouts  8.16 us
    ppermute x1, waiting for transfers between devices, local(): last = lax.ppermute(other, 'head', [(i, i ^ 2) for i in range(4)])  6.56 us
  transfers between devices with their start and end apart: 18, of which 2 were waited for; matrix products, arithmetic and copies ran while one was open for 0% of the time, Pallas kernels for 64%

profile of v1, /device:TPU:2, one launch (start us, length us, event | category | flops | bytes accessed | tf_op | source)
XLA Modules:
  0.0 222.9 jit_solution(15088636088033000115)
XLA Ops:
  0.0 0.9 copy-done.5
  0.9 0.9 copy-done.6
  1.8 0.7 copy-done.8
  2.4 0.7 copy-done.9
  3.1 0.7 copy-done.10
  3.8 0.3 prepare_queries.1.refs_0_
  4.1 3.4 %collective-permute-start.12 = (bf16[128,512]{1,0:T(8,128)(2,1)S(1)}, bf16[128,512]{1,0:T(8,128)(2,1)S(1)}, u32[]{:S(2)}, u32[]{:S(2)}) collective-permute-start(bf16[128,512]{1,0:T(8,128)(2,1)S(1)} %prepare_queries.1.refs_0_), channel_id=1, source_target_pairs={{0,16},{4,20},{8,24},{12,28},{16,32},{20,36},{24,40},{28,44},{32,4... | collective-permute-start | bytes 393224 | tf_op jit(solution)/shard_map/ppermute | solution.py:265
  7.4 3.1 %collective-permute-start.13 = (bf16[128,512]{1,0:T(8,128)(2,1)S(1)}, bf16[128,512]{1,0:T(8,128)(2,1)S(1)}, u32[]{:S(2)}, u32[]{:S(2)}) collective-permute-start(bf16[128,512]{1,0:T(8,128)(2,1)S(1)} %prepare_queries.1.refs_0_), channel_id=1, source_target_pairs={{0,240},{4,244},{8,248},{12,252},{16,0},{20,4},{24,8},{28,12},{32,... | collective-permute-start | bytes 393224 | tf_op jit(solution)/shard_map/ppermute | solution.py:265
  10.5 2.0 collective-permute-start.8
  12.6 3.9 %collective-permute-start.9 = (bf16[128,512]{1,0:T(8,128)(2,1)S(1)}, bf16[128,512]{1,0:T(8,128)(2,1)S(1)}, u32[]{:S(2)}, u32[]{:S(2)}) collective-permute-start(bf16[128,512]{1,0:T(8,128)(2,1)S(1)} %prepare_queries.1.refs_0_), channel_id=1, source_target_pairs={{0,244},{4,248},{8,252},{12,0},{16,4},{20,8},{24,12},{28,16},{32,2... | collective-permute-start | bytes 393224 | tf_op jit(solution)/shard_map/ppermute | solution.py:265
  16.5 1.0 collective-permute-start.4
  17.8 1.4 copy-done.2
  19.2 1.4 copy-done.3
  20.6 2.2 prepare_bins.1
  22.8 3.2 %collective-permute-start.5 = (bf16[128,512]{1,0:T(8,128)(2,1)S(1)}, bf16[128,512]{1,0:T(8,128)(2,1)S(1)}, u32[]{:S(2)}, u32[]{:S(2)}) collective-permute-start(bf16[128,512]{1,0:T(8,128)(2,1)S(1)} %prepare_queries.1.refs_0_), channel_id=1, source_target_pairs={{0,248},{4,252},{8,0},{12,4},{16,8},{20,12},{24,16},{28,20},{32,24... | collective-permute-start | bytes 393224 | tf_op jit(solution)/shard_map/ppermute | solution.py:265
  26.0 0.7 collective-permute-start
  26.7 7.4 %attend.9 = (bf16[128,512]{1,0:T(8,128)(2,1)S(1)}, bf16[128,512]{1,0:T(8,128)(2,1)S(1)}) custom-call(f32[4]{0:T(128)S(1)} %copy-done.7, s32[2]{0:T(128)S(1)} %add_convert_fusion.4.ok_ref, bf16[128,512]{1,0:T(8,128)(2,1)S(1)} %collective-permute-done.12.refs_0_, bf16[128,512]{1,0:T(8,128)(2,1)S(1)} %collective-permute-done.13.refs_1_, ...), custom_call_target="tpu_custom_call" | custom-call | flops 1073741824 | bytes 4194304 | tf_op jit(solution)/shard_map/attend/pallas_call | solution.py:191
  34.1 4.4 %collective-permute-start.1 = (bf16[128,512]{1,0:T(8,128)(2,1)S(1)}, bf16[128,512]{1,0:T(8,128)(2,1)S(1)}, u32[]{:S(2)}, u32[]{:S(2)}) collective-permute-start(bf16[128,512]{1,0:T(8,128)(2,1)S(1)} %prepare_queries.1.refs_0_), channel_id=1, source_target_pairs={{0,252},{4,0},{8,4},{12,8},{16,12},{20,16},{24,20},{28,24},{32,28}... | collective-permute-start | bytes 393224 | tf_op jit(solution)/shard_map/ppermute | solution.py:265
  38.6 7.4 %attend.8 = (bf16[128,512]{1,0:T(8,128)(2,1)S(1)}, bf16[128,512]{1,0:T(8,128)(2,1)S(1)}) custom-call(f32[4]{0:T(128)S(1)} %copy-done.7, s32[2]{0:T(128)S(1)} %add_convert_fusion.3.ok_ref, bf16[128,512]{1,0:T(8,128)(2,1)S(1)} %collective-permute-done.8.refs_0_, bf16[128,512]{1,0:T(8,128)(2,1)S(1)} %collective-permute-done.9.refs_1_, ...), custom_call_target="tpu_custom_call" | custom-call | flops 1073741824 | bytes 4194304 | tf_op jit(solution)/shard_map/attend/pallas_call | solution.py:191
  46.0 3.0 %collective-permute-start.15 = (bf16[128,512]{1,0:T(8,128)(2,1)S(1)}, bf16[128,512]{1,0:T(8,128)(2,1)S(1)}, u32[]{:S(2)}, u32[]{:S(2)}) collective-permute-start(bf16[128,512]{1,0:T(8,128)(2,1)S(1)} %get-tuple-element.26), channel_id=1, source_target_pairs={{0,16},{4,20},{8,24},{12,28},{16,32},{20,36},{24,40},{28,44},{32,4... | collective-permute-start | bytes 393224 | tf_op jit(solution)/shard_map/ppermute | solution.py:265
  49.0 15.7 %collective-permute-start.10 = (bf16[128,512]{1,0:T(8,128)(2,1)S(1)}, bf16[128,512]{1,0:T(8,128)(2,1)S(1)}, u32[]{:S(2)}, u32[]{:S(2)}) collective-permute-start(bf16[128,512]{1,0:T(8,128)(2,1)S(1)} %get-tuple-element.23), channel_id=1, source_target_pairs={{0,244},{4,248},{8,252},{12,0},{16,4},{20,8},{24,12},{28,16},{32,2... | collective-permute-start | bytes 393224 | tf_op jit(solution)/shard_map/ppermute | solution.py:265
  64.7 8.0 %attend.7 = (bf16[128,512]{1,0:T(8,128)(2,1)}, bf16[128,512]{1,0:T(8,128)(2,1)S(1)}) custom-call(f32[4]{0:T(128)S(1)} %copy-done.7, s32[2]{0:T(128)S(1)} %add_convert_fusion.2.ok_ref, bf16[128,512]{1,0:T(8,128)(2,1)S(1)} %collective-permute-done.4.refs_0_, bf16[128,512]{1,0:T(8,128)(2,1)S(1)} %collective-permute-done.5.refs_1_, ...), custom_call_target="tpu_custom_call" | custom-call | flops 1073741824 | bytes 4194304 | tf_op jit(solution)/shard_map/attend/pallas_call | solution.py:191
  72.8 78.4 %attend.6 = (bf16[128,512]{1,0:T(8,128)(2,1)}, bf16[128,512]{1,0:T(8,128)(2,1)}) custom-call(f32[4]{0:T(128)S(1)} %copy-done.7, s32[2]{0:T(128)S(1)} %add_convert_fusion.1.ok_ref, bf16[128,512]{1,0:T(8,128)(2,1)S(1)} %collective-permute-done.refs_0_, bf16[128,512]{1,0:T(8,128)(2,1)S(1)} %collective-permute-done.1.refs_1_, ...), custom_call_target="tpu_custom_call" | custom-call | flops 1073741824 | bytes 4194304 | tf_op jit(solution)/shard_map/attend/pallas_call | solution.py:191
  151.3 2.0 collective-permute-start.7
  153.2 4.5 %collective-permute-start.2 = (bf16[128,512]{1,0:T(8,128)(2,1)}, bf16[128,512]{1,0:T(8,128)(2,1)S(1)}, u32[]{:S(2)}, u32[]{:S(2)}) collective-permute-start(bf16[128,512]{1,0:T(8,128)(2,1)} %get-tuple-element.19), channel_id=1, source_target_pairs={{0,252},{4,0},{8,4},{12,8},{16,12},{20,16},{24,20},{28,24},{32,28}... | collective-permute-start | bytes 393224 | tf_op jit(solution)/shard_map/ppermute | solution.py:265
  157.7 1.6 copy-done.1
  159.3 40.1 %attend.5.refs_0_ = bf16[128,512]{1,0:T(8,128)(2,1)S(1)} custom-call(f32[4]{0:T(128)S(1)} %copy-done.7, s32[1]{0:T(128)} %constant.4.clone.1.ok_ref, bf16[128,512]{1,0:T(8,128)(2,1)S(1)} %prepare_queries.1.refs_0_, bf16[4,2048,128]{2,1,0:T(8,128)(2,1)S(1)} %get-tuple-element.17.refs_1_.refs_2_, bf16[4,2048,128]{2,1,0:T(8,128)(2,1)S(1)} %copy-done.1), custom_call_target="tpu_custom_call" | custom-call | flops 536870912 | bytes 4194304 | tf_op jit(solution)/shard_map/attend/pallas_call | solution.py:191
  199.5 1.7 merge.1
  201.2 13.3 %collective-permute-start.16 = (bf16[2,128,384]{2,1,0:T(8,128)(2,1)S(1)}, bf16[2,128,384]{2,1,0:T(8,128)(2,1)S(1)}, u32[]{:S(2)}, u32[]{:S(2)}) collective-permute-start(bf16[2,128,384]{2,1,0:T(8,128)(2,1)S(1)} %get-tuple-element.28), channel_id=1, source_target_pairs={{0,1},{1,0},{2,3},{3,2},{4,5},{5,4},{6,7},{7,6},{8,9},{9,8},{10,11... | collective-permute-start | bytes 589832 | tf_op jit(solution)/shard_map/ppermute | solution.py:284
  214.4 1.1 collective-permute-done.16
  215.6 6.6 %collective-permute-done.17 = bf16[128,384]{1,0:T(8,128)(2,1)S(1)} collective-permute-done((bf16[128,384]{1,0:T(8,128)(2,1)S(1)}, bf16[128,384]{1,0:T(8,128)(2,1)S(1)}, u32[]{:S(2)}, u32[]{:S(2)}) %collective-permute-start.17) | collective-permute-done | bytes 98336 | tf_op jit(solution)/shard_map/ppermute | solution.py:286
  222.2 0.7 fusion
  (40 shorter events, 0.6 us)
Async XLA Ops:
  0.0 0.9 copy-start.5
  0.9 0.9 copy-start.6
  1.8 0.7 copy-start.8
  2.4 0.7 copy-start.9
  3.1 0.7 copy-start.10
  4.1 18.7 %collective-permute-start.12 = (bf16[128,512]{1,0:T(8,128)(2,1)S(1)}, bf16[128,512]{1,0:T(8,128)(2,1)S(1)}, u32[]{:S(2)}, u32[]{:S(2)}) collective-permute-start(bf16[128,512]{1,0:T(8,128)(2,1)S(1)} %prepare_queries.1.refs_0_), channel_id=1, source_target_pairs={{0,16},{4,20},{8,24},{12,28},{16,32},{20,36},{24,40},{28,44},{32,4... | collective-permute-start | bytes 393224 | tf_op jit(solution)/shard_map/ppermute | solution.py:265
  7.4 18.6 %collective-permute-start.13 = (bf16[128,512]{1,0:T(8,128)(2,1)S(1)}, bf16[128,512]{1,0:T(8,128)(2,1)S(1)}, u32[]{:S(2)}, u32[]{:S(2)}) collective-permute-start(bf16[128,512]{1,0:T(8,128)(2,1)S(1)} %prepare_queries.1.refs_0_), channel_id=1, source_target_pairs={{0,240},{4,244},{8,248},{12,252},{16,0},{20,4},{24,8},{28,12},{32,... | collective-permute-start | bytes 393224 | tf_op jit(solution)/shard_map/ppermute | solution.py:265
  10.5 23.6 %collective-permute-start.8 = (bf16[128,512]{1,0:T(8,128)(2,1)S(1)}, bf16[128,512]{1,0:T(8,128)(2,1)S(1)}, u32[]{:S(2)}, u32[]{:S(2)}) collective-permute-start(bf16[128,512]{1,0:T(8,128)(2,1)S(1)} %prepare_queries.1.refs_0_), channel_id=1, source_target_pairs={{0,12},{4,16},{8,20},{12,24},{16,28},{20,32},{24,36},{28,40},{32,4... | collective-permute-start | bytes 393224 | tf_op jit(solution)/shard_map/ppermute | solution.py:265
  12.6 26.0 %collective-permute-start.9 = (bf16[128,512]{1,0:T(8,128)(2,1)S(1)}, bf16[128,512]{1,0:T(8,128)(2,1)S(1)}, u32[]{:S(2)}, u32[]{:S(2)}) collective-permute-start(bf16[128,512]{1,0:T(8,128)(2,1)S(1)} %prepare_queries.1.refs_0_), channel_id=1, source_target_pairs={{0,244},{4,248},{8,252},{12,0},{16,4},{20,8},{24,12},{28,16},{32,2... | collective-permute-start | bytes 393224 | tf_op jit(solution)/shard_map/ppermute | solution.py:265
  16.5 29.6 %collective-permute-start.4 = (bf16[128,512]{1,0:T(8,128)(2,1)S(1)}, bf16[128,512]{1,0:T(8,128)(2,1)S(1)}, u32[]{:S(2)}, u32[]{:S(2)}) collective-permute-start(bf16[128,512]{1,0:T(8,128)(2,1)S(1)} %prepare_queries.1.refs_0_), channel_id=1, source_target_pairs={{0,8},{4,12},{8,16},{12,20},{16,24},{20,28},{24,32},{28,36},{32,40... | collective-permute-start | bytes 393224 | tf_op jit(solution)/shard_map/ppermute | solution.py:265
  17.8 1.4 copy-start.2
  19.2 1.4 copy-start.3
  20.6 6.1 %copy-start.7 = (f32[4]{0:T(128)S(1)}, f32[4]{0:T(128)}, u32[]{:S(2)}) copy-start(f32[4]{0:T(128)} %slopes_ref.9) | copy-start | bytes 52
  22.8 50.1 %copy-start = (bf16[4,2048,128]{2,1,0:T(8,128)(2,1)}, bf16[4,2048,128]{2,1,0:T(8,128)(2,1)S(1)}, u32[]{:S(2)}) copy-start(bf16[4,2048,128]{2,1,0:T(8,128)(2,1)S(1)} %get-tuple-element.18.refs_2_.refs_3_) | copy-start | bytes 6291460
  22.8 26.2 %collective-permute-start.5 = (bf16[128,512]{1,0:T(8,128)(2,1)S(1)}, bf16[128,512]{1,0:T(8,128)(2,1)S(1)}, u32[]{:S(2)}, u32[]{:S(2)}) collective-permute-start(bf16[128,512]{1,0:T(8,128)(2,1)S(1)} %prepare_queries.1.refs_0_), channel_id=1, source_target_pairs={{0,248},{4,252},{8,0},{12,4},{16,8},{20,12},{24,16},{28,20},{32,24... | collective-permute-start | bytes 393224 | tf_op jit(solution)/shard_map/ppermute | solution.py:265
  26.0 46.7 %collective-permute-start = (bf16[128,512]{1,0:T(8,128)(2,1)S(1)}, bf16[128,512]{1,0:T(8,128)(2,1)S(1)}, u32[]{:S(2)}, u32[]{:S(2)}) collective-permute-start(bf16[128,512]{1,0:T(8,128)(2,1)S(1)} %prepare_queries.1.refs_0_), channel_id=1, source_target_pairs={{0,4},{4,8},{8,12},{12,16},{16,20},{20,24},{24,28},{28,32},{32,36}... | collective-permute-start | bytes 393224 | tf_op jit(solution)/shard_map/ppermute | solution.py:265
  34.1 38.6 %collective-permute-start.1 = (bf16[128,512]{1,0:T(8,128)(2,1)S(1)}, bf16[128,512]{1,0:T(8,128)(2,1)S(1)}, u32[]{:S(2)}, u32[]{:S(2)}) collective-permute-start(bf16[128,512]{1,0:T(8,128)(2,1)S(1)} %prepare_queries.1.refs_0_), channel_id=1, source_target_pairs={{0,252},{4,0},{8,4},{12,8},{16,12},{20,16},{24,20},{28,24},{32,28}... | collective-permute-start | bytes 393224 | tf_op jit(solution)/shard_map/ppermute | solution.py:265
  38.6 112.7 %collective-permute-start.14 = (bf16[128,512]{1,0:T(8,128)(2,1)S(1)}, bf16[128,512]{1,0:T(8,128)(2,1)S(1)}, u32[]{:S(2)}, u32[]{:S(2)}) collective-permute-start(bf16[128,512]{1,0:T(8,128)(2,1)S(1)} %get-tuple-element.25), channel_id=1, source_target_pairs={{0,240},{4,244},{8,248},{12,252},{16,0},{20,4},{24,8},{28,12},{32,... | collective-permute-start | bytes 393224 | tf_op jit(solution)/shard_map/ppermute | solution.py:265
  46.0 107.2 %collective-permute-start.15 = (bf16[128,512]{1,0:T(8,128)(2,1)S(1)}, bf16[128,512]{1,0:T(8,128)(2,1)S(1)}, u32[]{:S(2)}, u32[]{:S(2)}) collective-permute-start(bf16[128,512]{1,0:T(8,128)(2,1)S(1)} %get-tuple-element.26), channel_id=1, source_target_pairs={{0,16},{4,20},{8,24},{12,28},{16,32},{20,36},{24,40},{28,44},{32,4... | collective-permute-start | bytes 393224 | tf_op jit(solution)/shard_map/ppermute | solution.py:265
  49.0 108.7 %collective-permute-start.10 = (bf16[128,512]{1,0:T(8,128)(2,1)S(1)}, bf16[128,512]{1,0:T(8,128)(2,1)S(1)}, u32[]{:S(2)}, u32[]{:S(2)}) collective-permute-start(bf16[128,512]{1,0:T(8,128)(2,1)S(1)} %get-tuple-element.23), channel_id=1, source_target_pairs={{0,244},{4,248},{8,252},{12,0},{16,4},{20,8},{24,12},{28,16},{32,2... | collective-permute-start | bytes 393224 | tf_op jit(solution)/shard_map/ppermute | solution.py:265
  72.7 126.7 %collective-permute-start.11 = (bf16[128,512]{1,0:T(8,128)(2,1)S(1)}, bf16[128,512]{1,0:T(8,128)(2,1)S(1)}, u32[]{:S(2)}, u32[]{:S(2)}) collective-permute-start(bf16[128,512]{1,0:T(8,128)(2,1)S(1)} %get-tuple-element.24), channel_id=1, source_target_pairs={{0,12},{4,16},{8,20},{12,24},{16,28},{20,32},{24,36},{28,40},{32,4... | collective-permute-start | bytes 393224 | tf_op jit(solution)/shard_map/ppermute | solution.py:265
  72.7 126.7 %collective-permute-start.6 = (bf16[128,512]{1,0:T(8,128)(2,1)}, bf16[128,512]{1,0:T(8,128)(2,1)S(1)}, u32[]{:S(2)}, u32[]{:S(2)}) collective-permute-start(bf16[128,512]{1,0:T(8,128)(2,1)} %get-tuple-element.21), channel_id=1, source_target_pairs={{0,248},{4,252},{8,0},{12,4},{16,8},{20,12},{24,16},{28,20},{32,24... | collective-permute-start | bytes 393224 | tf_op jit(solution)/shard_map/ppermute | solution.py:265
  151.3 48.2 %collective-permute-start.7 = (bf16[128,512]{1,0:T(8,128)(2,1)S(1)}, bf16[128,512]{1,0:T(8,128)(2,1)S(1)}, u32[]{:S(2)}, u32[]{:S(2)}) collective-permute-start(bf16[128,512]{1,0:T(8,128)(2,1)S(1)} %get-tuple-element.22), channel_id=1, source_target_pairs={{0,8},{4,12},{8,16},{12,20},{16,24},{20,28},{24,32},{28,36},{32,40... | collective-permute-start | bytes 393224 | tf_op jit(solution)/shard_map/ppermute | solution.py:265
  153.2 46.2 %collective-permute-start.2 = (bf16[128,512]{1,0:T(8,128)(2,1)}, bf16[128,512]{1,0:T(8,128)(2,1)S(1)}, u32[]{:S(2)}, u32[]{:S(2)}) collective-permute-start(bf16[128,512]{1,0:T(8,128)(2,1)} %get-tuple-element.19), channel_id=1, source_target_pairs={{0,252},{4,0},{8,4},{12,8},{16,12},{20,16},{24,20},{28,24},{32,28}... | collective-permute-start | bytes 393224 | tf_op jit(solution)/shard_map/ppermute | solution.py:265
  157.7 41.8 %collective-permute-start.3 = (bf16[128,512]{1,0:T(8,128)(2,1)}, bf16[128,512]{1,0:T(8,128)(2,1)S(1)}, u32[]{:S(2)}, u32[]{:S(2)}) collective-permute-start(bf16[128,512]{1,0:T(8,128)(2,1)} %get-tuple-element.20), channel_id=1, source_target_pairs={{0,4},{4,8},{8,12},{12,16},{16,20},{20,24},{24,28},{28,32},{32,36}... | collective-permute-start | bytes 393224 | tf_op jit(solution)/shard_map/ppermute | solution.py:265
  157.7 1.6 copy-start.1
  159.3 40.2 %copy-start.4 = (bf16[384,1536]{1,0:T(8,128)(2,1)S(1)}, bf16[384,1536]{1,0:T(8,128)(2,1)}, u32[]{:S(2)}) copy-start(bf16[384,1536]{1,0:T(8,128)(2,1)} %refs_9_.1) | copy-start | bytes 3538948
  201.2 14.3 %collective-permute-start.16 = (bf16[2,128,384]{2,1,0:T(8,128)(2,1)S(1)}, bf16[2,128,384]{2,1,0:T(8,128)(2,1)S(1)}, u32[]{:S(2)}, u32[]{:S(2)}) collective-permute-start(bf16[2,128,384]{2,1,0:T(8,128)(2,1)S(1)} %get-tuple-element.28), channel_id=1, source_target_pairs={{0,1},{1,0},{2,3},{3,2},{4,5},{5,4},{6,7},{7,6},{8,9},{9,8},{10,11... | collective-permute-start | bytes 589832 | tf_op jit(solution)/shard_map/ppermute | solution.py:284
  215.5 6.7 %collective-permute-start.17 = (bf16[128,384]{1,0:T(8,128)(2,1)S(1)}, bf16[128,384]{1,0:T(8,128)(2,1)S(1)}, u32[]{:S(2)}, u32[]{:S(2)}) collective-permute-start(bf16[128,384]{1,0:T(8,128)(2,1)S(1)} %fusion.1), channel_id=1, source_target_pairs={{0,2},{1,3},{2,0},{3,1},{4,6},{5,7},{6,4},{7,5},{8,10},{9,11},{10,... | collective-permute-start | bytes 294920 | tf_op jit(solution)/shard_map/ppermute | solution.py:286

commit v2 on v1

v2 whole, which is shorter than its diff:
```python
import functools
import math

import jax
import jax.numpy as jnp
from jax import lax
from jax.experimental import pallas as pl
from jax.experimental.pallas import tpu as pltpu
from jax.sharding import PartitionSpec as P

HEAD_DIM = 96
RADIUS = 7812
SHIFT = 64
LANES = 128
LOG2E = math.log2(math.e)
SCALE2 = LOG2E / math.sqrt(HEAD_DIM)
FAR = 1e30
EMPTY = -16384.0
SUM_LO, SUM_HI = 2.0**-60, 2.0**100
TILE = 512
QUERY_VMEM = 4 * 2**20
BINS_VMEM = 16 * 2**20
OVER_ROWS = (((1,), (1,)), ((), ()))

SMEM = pl.BlockSpec(memory_space=pltpu.SMEM)
VMEM = pl.BlockSpec(memory_space=pltpu.VMEM)
HBM = pl.BlockSpec(memory_space=pltpu.HBM)


def column(row):
    n = row.shape[1]
    eye = lax.broadcasted_iota(jnp.int32, (n, n), 0) == lax.broadcasted_iota(jnp.int32, (n, n), 1)
    return jnp.sum(jnp.where(eye, row, 0.0), axis=1, keepdims=True)


def query_kernel(groups, base_ref, *refs):
    sources, out_ref, copies, sems = refs[:5], refs[5], refs[6:11], refs[11]
    moves = [pltpu.make_async_copy(a, b, sems.at[i]) for i, (a, b) in enumerate(zip(sources, copies))]
    for move in moves:
        move.start()
    for move in moves:
        move.wait()
    types_ref, promoters_ref, offsets_ref, queries_ref, embed_ref = copies
    rows = queries_ref.shape[0]
    kinds = embed_ref.shape[0]
    one_hot = (lax.broadcasted_iota(jnp.int32, (kinds, rows), 0) == types_ref[...]).astype(jnp.float32)
    embedded = jnp.dot(one_hot.T.astype(jnp.bfloat16), embed_ref[...], preferred_element_type=jnp.float32)
    query = (queries_ref[...].astype(jnp.float32) + embedded).astype(jnp.bfloat16)
    place = promoters_ref[...] + offsets_ref[...] - base_ref[0] + SHIFT
    coarse = lax.shift_right_arithmetic(place, 4)
    fine = place - coarse * 16
    coarse = column((coarse * 16).astype(jnp.float32))
    fine = column(fine.astype(jnp.float32))
    lane = lax.broadcasted_iota(jnp.int32, (rows, LANES - HEAD_DIM), 1)
    extra = jnp.where(lane == 0, coarse, jnp.where(lane == 1, fine, 0.0)).astype(jnp.bfloat16)
    for g in range(groups):
        out_ref[:, g * LANES : g * LANES + HEAD_DIM] = query[:, g * HEAD_DIM : (g + 1) * HEAD_DIM]
        out_ref[:, g * LANES + HEAD_DIM : (g + 1) * LANES] = extra


def spread(groups, keys, values, keys_out, values_out):
    count = keys.shape[0]
    lane = lax.broadcasted_iota(jnp.int32, (count, LANES - HEAD_DIM), 1)
    blank = jnp.zeros((count, LANES - HEAD_DIM), jnp.bfloat16)
    ones = jnp.where(lane == 0, 1.0, 0.0).astype(jnp.bfloat16)
    for g in range(groups):
        columns = slice(g * HEAD_DIM, (g + 1) * HEAD_DIM)
        keys_out[g] = jnp.concatenate([keys[:, columns], blank], axis=1)
        values_out[g] = jnp.concatenate([values[:, columns], ones], axis=1)


def block_facts(query, strides, stride, bins, ok):
    extra = query[:, HEAD_DIM:LANES].astype(jnp.float32)
    centre = extra[:, 0:1] + extra[:, 1:2] - (stride * bins + SHIFT).astype(jnp.float32)
    before, after = -centre, centre - float(bins - 1)
    if strides == (0,):
        base = jnp.zeros_like(centre)
    elif min(strides) > 0:
        base = before
    elif max(strides) < 0:
        base = after
    else:
        base = jnp.maximum(before, after)
    return centre, base, (jnp.maximum(before, after) <= RADIUS) & (ok > 0)


def tile_needs(strides, bins, start, size):
    bends, ends = min(strides) <= 0 <= max(strides), False
    for stride in strides:
        low, high = -SHIFT - stride * bins, bins - 1 + SHIFT - stride * bins
        if max(-high, low - (bins - 1)) > RADIUS:
            continue
        if stride >= 0:
            bends |= high > start
            ends |= start + size - 1 - low > RADIUS
        if stride <= 0:
            bends |= low < start + size - 1
            ends |= high - start > RADIUS
    bends |= min(strides) < 0 < max(strides)
    return bends, ends


def attend_rows(blocks, strides, oks, slopes, query_refs, keys_ref, values_ref, out_refs, acc_ref):
    groups, bins, _ = keys_ref.shape
    rows = query_refs[0].shape[0]
    n = len(query_refs)
    parts = [slice(i * rows, (i + 1) * rows) for i in range(n)]
    facts = [block_facts(ref[:, :LANES], block, stride, bins, ok) for ref, block, stride, ok in zip(query_refs, blocks, strides, oks)]
    centre, base = (jnp.concatenate([fact[k] for fact in facts], axis=0) for k in range(2))
    alive = jnp.concatenate([jnp.where(fact[2], 1.0, 0.0) for fact in facts], axis=0) > 0.0

    def queries(g):
        return jnp.concatenate([ref[:, g * LANES : (g + 1) * LANES] for ref in query_refs], axis=0)

    def products(g, start, size):
        keys = keys_ref[g, pl.ds(start, size), :]
        return lax.dot_general(queries(g), keys, OVER_ROWS, preferred_element_type=jnp.float32)

    def positions(start, size):
        return (start + lax.broadcasted_iota(jnp.int32, (1, size), 1)).astype(jnp.float32)

    def finish(g, acc, shift):
        lane = lax.broadcasted_iota(jnp.int32, acc.shape, 1)
        exponent = shift - slopes[g] * base
        coarse = jnp.where(alive, jnp.round(exponent * 0.0625) * 16.0, EMPTY)
        scaled = jnp.where(alive, acc * jnp.exp2(exponent - coarse), 0.0)
        total = scaled[:, HEAD_DIM : HEAD_DIM + 1]
        high = total.astype(jnp.bfloat16).astype(jnp.float32)
        scaled = jnp.where(lane == HEAD_DIM + 1, total - high, scaled)
        scaled = jnp.where(lane == HEAD_DIM + 2, coarse, scaled).astype(jnp.bfloat16)
        for part, ref in zip(parts, out_refs):
            ref[:, g * LANES : (g + 1) * LANES] = scaled[part]

    accs = [jnp.zeros((n * rows, LANES), jnp.float32)] * groups
    for start in range(0, bins, TILE):
        position = positions(start, TILE)
        shapes = []
        for block, (middle, origin, _) in zip(blocks, facts):
            bends, ends = tile_needs(block, bins, start, TILE)
            if bends:
                distance = jnp.abs(position - middle) - origin
            else:
                distance = position if min(block) > 0 else float(bins - 1) - position
            usable = None
            if ends:
                usable = jnp.abs(position - middle) <= RADIUS
            shapes.append((distance, usable))
        for g in range(groups):
            raw = products(g, start, TILE)
            weights = []
            for part, (distance, usable) in zip(parts, shapes):
                weight = jnp.exp2(raw[part] * SCALE2 - slopes[g] * distance)
                weights.append(weight if usable is None else jnp.where(usable, weight, 0.0))
            weights = jnp.concatenate([weight.astype(jnp.bfloat16) for weight in weights], axis=0)
            accs[g] += jnp.dot(weights, values_ref[g, start : start + TILE, :], preferred_element_type=jnp.float32)
    wrong = jnp.zeros((n * rows, 1), jnp.float32)
    for g in range(groups):
        total = accs[g][:, HEAD_DIM : HEAD_DIM + 1]
        wrong = jnp.where((total >= SUM_LO) & (total <= SUM_HI), wrong, 1.0)
        finish(g, accs[g], 0.0)

    @pl.when(jnp.max(jnp.where(alive, wrong, 0.0)) > 0.0)
    def _():
        for g in range(groups):

            def logs(k):
                start = pl.multiple_of(k * LANES, LANES)
                distance = jnp.abs(positions(start, LANES) - centre)
                exponent = products(g, start, LANES) * SCALE2 - slopes[g] * (distance - base)
                return start, jnp.where(distance <= RADIUS, exponent, -FAR)

            def largest(k, so_far):
                return jnp.maximum(so_far, jnp.max(logs(k)[1], axis=1, keepdims=True))

            shift = lax.fori_loop(0, bins // LANES, largest, jnp.full((n * rows, 1), -FAR, jnp.float32))
            acc_ref[...] = jnp.zeros_like(acc_ref)

            @pl.loop(0, bins // LANES)
            def _(k):
                start, exponent = logs(k)
                weights = jnp.exp2(exponent - shift).astype(jnp.bfloat16)
                acc_ref[...] += jnp.dot(weights, values_ref[g, pl.ds(start, LANES), :], preferred_element_type=jnp.float32)

            finish(g, acc_ref[...], shift)


def near_kernel(blocks, slopes_ref, facts_ref, *refs):
    n = len(blocks)
    query_refs, (keys_ref, values_ref, out_ref, acc_ref) = refs[:-4], refs[-4:]
    groups = keys_ref.shape[0]
    rows = out_ref.shape[0] // n
    slices = [pl.ds(i * rows, rows) for i in range(n)]
    if len(query_refs) == 1:
        query_refs = [query_refs[0].at[rows_of] for rows_of in slices]
    attend_rows(
        blocks,
        [facts_ref[2 * i] for i in range(n)],
        [facts_ref[2 * i + 1] for i in range(n)],
        [slopes_ref[g] * LOG2E for g in range(groups)],
        query_refs,
        keys_ref,
        values_ref,
        [out_ref.at[rows_of] for rows_of in slices],
        acc_ref,
    )


def bins_kernel(groups, keys_ref, values_ref, keys_out, values_out):
    spread(groups, keys_ref[...], values_ref[...], keys_out, values_out)


def combined(parts):
    parts = [part.astype(jnp.float32) for part in parts]
    scales = [part[:, HEAD_DIM + 2 : HEAD_DIM + 3] for part in parts]
    top = functools.reduce(jnp.maximum, scales)
    acc = sum(part * jnp.exp2(scale - top) for part, scale in zip(parts, scales))
    return acc, acc[:, HEAD_DIM : HEAD_DIM + 1] + acc[:, HEAD_DIM + 1 : HEAD_DIM + 2], top


def other_kernel(groups, *refs):
    part_refs, out_ref = refs[:-1], refs[-1]
    rows = out_ref.shape[0]
    lane = lax.broadcasted_iota(jnp.int32, (rows, LANES), 1)
    for g in range(groups):
        lanes = slice(g * LANES, (g + 1) * LANES)
        acc, total, top = combined([ref[rows:, lanes] for ref in part_refs])
        high = total.astype(jnp.bfloat16).astype(jnp.float32)
        acc = jnp.where(lane == HEAD_DIM, high, jnp.where(lane == HEAD_DIM + 1, total - high, acc))
        acc = jnp.where(lane == HEAD_DIM + 2, top, acc)
        out_ref[:, lanes] = acc.astype(jnp.bfloat16)


def merge_kernel(groups, place_ref, *refs):
    part_refs, (w_ref, keep_ref, send_ref) = refs[:-3], refs[-3:]
    rows = part_refs[0].shape[0]
    pooled = []
    for g in range(groups):
        acc, total, _ = combined([ref[:rows, g * LANES : (g + 1) * LANES] for ref in part_refs])
        pooled.append((acc[:, :HEAD_DIM] / total).astype(jnp.bfloat16))
    width = w_ref.shape[1] // 4
    core, high = place_ref[0] & 1, place_ref[0] >> 1
    for k in range(2):
        row = jnp.where(k == 0, high, 1 - high) * 2
        for ref, lane in ((send_ref, 1 - core), (keep_ref, core)):
            start = pl.multiple_of((row + lane) * width, LANES)
            acc = jnp.zeros((rows, width), jnp.float32)
            for g in range(groups):
                weights = w_ref[g * HEAD_DIM : (g + 1) * HEAD_DIM, pl.ds(start, width)]
                acc += jnp.dot(pooled[g], weights, preferred_element_type=jnp.float32)
            ref[k] = acc.astype(ref.dtype)


def attend_cost(rows, bins, groups):
    return pl.CostEstimate(
        flops=4 * rows * bins * groups * LANES, bytes_accessed=4 * 2**20, transcendentals=rows * bins * groups
    )


def prepare_queries(queries, cell_types, promoters, offsets, cell_embed, base, groups):
    rows = queries.shape[0]
    sources = [cell_types[None, :], promoters[None, :], offsets[None, :], queries, cell_embed]
    return pl.pallas_call(
        functools.partial(query_kernel, groups),
        in_specs=[SMEM] + [HBM] * 5,
        out_specs=VMEM,
        out_shape=jax.ShapeDtypeStruct((rows, groups * LANES), jnp.bfloat16),
        scratch_shapes=[pltpu.VMEM(a.shape, a.dtype) for a in sources] + [pltpu.SemaphoreType.DMA((5,))],
        compiler_params=pltpu.CompilerParams(vmem_limit_bytes=QUERY_VMEM),
        name="prepare_queries",
    )(base[None], *sources)


def prepare_bins(keys, values, groups):
    bins = keys.shape[0]
    step = 256
    flat = pl.BlockSpec((step, keys.shape[1]), lambda i: (i, 0))
    split = pl.BlockSpec((groups, step, LANES), lambda i: (0, i, 0))
    return pl.pallas_call(
        functools.partial(bins_kernel, groups),
        grid=(bins // step,),
        in_specs=[flat, flat],
        out_specs=[split, split],
        out_shape=[jax.ShapeDtypeStruct((groups, bins, LANES), jnp.bfloat16)] * 2,
        compiler_params=pltpu.CompilerParams(vmem_limit_bytes=BINS_VMEM),
        cost_estimate=pl.CostEstimate(flops=0, bytes_accessed=7 * 2**20, transcendentals=0),
        name="prepare_bins",
    )(keys, values)


def attend_near(blocks, slopes, facts, queries, keys, values):
    groups, bins, _ = keys.shape
    width = queries[0].shape[1]
    rows = sum(query.shape[0] for query in queries)
    return pl.pallas_call(
        functools.partial(near_kernel, blocks),
        in_specs=[SMEM, SMEM] + [VMEM] * (len(queries) + 2),
        out_specs=VMEM,
        out_shape=jax.ShapeDtypeStruct((rows, width), jnp.bfloat16),
        scratch_shapes=[pltpu.VMEM((rows, LANES), jnp.float32)],
        compiler_params=pltpu.CompilerParams(vmem_limit_bytes=24 * 2**20),
        cost_estimate=attend_cost(rows, bins, groups),
        name="attend_near",
    )(slopes, facts, *queries, keys, values)


def merge_other(parts, groups):
    rows, width = parts[0].shape
    return pl.pallas_call(
        functools.partial(other_kernel, groups),
        in_specs=[VMEM] * len(parts),
        out_specs=VMEM,
        out_shape=jax.ShapeDtypeStruct((rows // 2, width), jnp.bfloat16),
        compiler_params=pltpu.CompilerParams(vmem_limit_bytes=8 * 2**20),
        name="merge_other",
    )(*parts)


def merge(place, parts, w_out, groups):
    rows = parts[0].shape[0]
    width = w_out.shape[1] // 4
    return pl.pallas_call(
        functools.partial(merge_kernel, groups),
        in_specs=[SMEM] + [VMEM] * (len(parts) + 1),
        out_specs=[VMEM] * 2,
        out_shape=[
            jax.ShapeDtypeStruct((2, rows, width), jnp.float32),
            jax.ShapeDtypeStruct((2, rows, width), jnp.bfloat16),
        ],
        compiler_params=pltpu.CompilerParams(vmem_limit_bytes=12 * 2**20),
        name="merge",
    )(place[None], *parts, w_out)


def rotated(value, steps):
    count = lax.axis_size("seq")
    return lax.ppermute(value, "seq", [(i, (i + steps) % count) for i in range(count)])


def swapped(value, axis, bit):
    return lax.ppermute(value, axis, [(i, i ^ bit) for i in range(lax.axis_size(axis))])


def local(queries, cell_types, promoters, offsets, cell_embed, bin_keys, bin_values, slopes, w_out):
    seq_count = lax.axis_size("seq")
    position = lax.axis_index("seq")
    place = lax.axis_index("head")
    bins = bin_keys.shape[0]
    groups = slopes.shape[0]
    odd = position & 1

    def facts(pairs):
        found = []
        for shift, same in pairs:
            stride = 2 * shift if same else 2 * shift + 2 * odd - 1
            block = position - stride
            found += [stride + 0 * odd, ((block >= 0) & (block < seq_count)).astype(jnp.int32)]
        return jnp.stack(found).astype(jnp.int32)

    mine = prepare_queries(queries, cell_types, promoters, offsets, cell_embed, position * bins, groups)
    other = swapped(mine, "seq", 1)
    keys, values = prepare_bins(bin_keys, bin_values, groups)
    other, keys, values = lax.optimization_barrier((other, keys, values))
    both = jnp.concatenate([mine, other], axis=0)
    shifts = [2, -2, 1, -1]
    arrived = [rotated(both, 2 * shift) for shift in shifts]
    part = attend_near(
        ((0,), (-1, 1)), slopes, facts([(0, True), (0, False)]), [mine, other], keys, values
    )
    parts = [part]
    for k in (2, 3, 0, 1):
        shift = shifts[k]
        query, _ = lax.optimization_barrier((arrived[k], part))
        part = attend_near(
            ((2 * shift,), (2 * shift - 1, 2 * shift + 1)), slopes, facts([(shift, True), (shift, False)]), [query], keys, values
        )
        parts.append(rotated(part, -2 * shift))
    theirs = swapped(merge_other(parts, groups), "seq", 1)
    keep, send = merge(place, [theirs] + parts, w_out, groups)
    got = swapped(send, "head", 1)
    rest = (keep[1] + got[1].astype(jnp.float32)).astype(jnp.bfloat16)
    last = swapped(rest, "head", 2)
    return (keep[0] + got[0].astype(jnp.float32) + last.astype(jnp.float32)).astype(jnp.bfloat16)


def solution(mesh):
    return jax.shard_map(
        local,
        mesh=mesh,
        in_specs=(
            P("seq", "head"),
            P("seq"),
            P("seq"),
            P("seq"),
            P(None, "head"),
            P("seq", "head"),
            P("seq", "head"),
            P("head"),
            P("head", None),
        ),
        out_specs=P("seq", "head"),
        check_vma=False,
    )
```

time: 227 us -> 193 us (0.85)
  waiting for transfers between devices: 7.67 us -> 89.5 us
  Pallas kernels: 146 us -> 65.6 us
  starting transfers between devices: 60.3 us -> 23.9 us
    pallas_call x6 -> x7, Pallas kernels: 142 us -> 62.1 us  [the longest x5 60.5 us: attend_near(): pl.pallas_call(functools.partial(near_kernel, blocks), in_specs=[SMEM, SM...]
    ppermute x16 -> x8, waiting for transfers between devices: 0.04 us -> 78.6 us  [rotated(): lax.ppermute(value, 'seq', [(i, (i + steps) % count) for i in range(count)])]
    ppermute x16 -> x8, starting transfers between devices: 47 us -> 20.2 us  [rotated(): lax.ppermute(value, 'seq', [(i, (i + steps) % count) for i in range(count)])]
    ppermute x2 -> x4, starting transfers between devices: 13.4 us -> 3.68 us  [swapped(): lax.ppermute(value, axis, [(i, i ^ bit) for i in range(lax.axis_size(axis...]
    ppermute x2 -> x4, waiting for transfers between devices: 7.63 us -> 11 us  [swapped(): lax.ppermute(value, axis, [(i, i ^ bit) for i in range(lax.axis_size(axis...]
  transfers between devices with their start and end apart: 18 -> 12, of which waited for: 2 -> 6; matrix products, arithmetic and copies ran while one was open for 0% -> 0% of each run, Pallas kernels for 64% -> 31%
where the time goes in v2:
time: 193 us; the launch traced here: 190 us
  waiting for transfers between devices  89.5 us (46%)
  Pallas kernels  65.6 us (34%)
  starting transfers between devices  23.9 us (12%)
  local copies, waits for them, and re-layouts  9.5 us (5%)
    ppermute x8, waiting for transfers between devices, rotated(): lax.ppermute(value, 'seq', [(i, (i + steps) % count) for i in range(count)])  78.6 us
    pallas_call x5, Pallas kernels, attend_near(): pl.pallas_call(functools.partial(near_kernel, blocks), in_specs=[SMEM, SM...  60.5 us
    ppermute x8, starting transfers between devices, rotated(): lax.ppermute(value, 'seq', [(i, (i + steps) % count) for i in range(count)])  20.2 us
    ppermute x4, waiting for transfers between devices, swapped(): lax.ppermute(value, axis, [(i, i ^ bit) for i in range(lax.axis_size(axis...  11 us
    unnamed x22, local copies, waits for them, and re-layouts  9.5 us
  transfers between devices with their start and end apart: 12, of which 6 were waited for; matrix products, arithmetic and copies ran while one was open for 0% of the time, Pallas kernels for 31%

profile of v2, /device:TPU:2, one launch (start us, length us, event | category | flops | bytes accessed | tf_op | source)
XLA Modules:
  0.0 189.8 jit_solution(6501740284974326966)
XLA Ops:
  0.0 0.9 copy-done.5
  0.9 0.9 copy-done.6
  1.8 0.7 copy-done.8
  2.4 0.7 copy-done.9
  3.1 0.7 copy-done.10
  3.8 0.6 prepare_queries.1.refs_0_
  4.4 1.7 collective-permute-start
  6.2 1.4 copy-done.2
  7.6 1.4 copy-done.3
  9.0 2.2 %prepare_bins.1 = (bf16[4,2048,128]{2,1,0:T(8,128)(2,1)S(1)}, bf16[4,2048,128]{2,1,0:T(8,128)(2,1)S(1)}) custom-call(bf16[2048,384]{1,0:T(8,128)(2,1)S(1)} %copy-done.2, bf16[2048,384]{1,0:T(8,128)(2,1)S(1)} %copy-done.3), custom_call_target="tpu_custom_call" | custom-call | bytes 7340032 | tf_op jit(solution)/shard_map/prepare_bins/pallas_call | solution.py:278
  11.2 1.3 copy-done
  12.7 2.0 %collective-permute-start.1 = (bf16[256,512]{1,0:T(8,128)(2,1)S(1)}, bf16[256,512]{1,0:T(8,128)(2,1)S(1)}, u32[]{:S(2)}, u32[]{:S(2)}) collective-permute-start(bf16[256,512]{1,0:T(8,128)(2,1)S(1)} %pad_maximum_fusion), channel_id=1, source_target_pairs={{0,8},{4,12},{8,16},{12,20},{16,24},{20,28},{24,32},{28,36},{32,40... | collective-permute-start | bytes 786440 | tf_op jit(solution)/shard_map/ppermute | solution.py:336
  14.8 4.0 %collective-permute-start.3 = (bf16[256,512]{1,0:T(8,128)(2,1)S(1)}, bf16[256,512]{1,0:T(8,128)(2,1)S(1)}, u32[]{:S(2)}, u32[]{:S(2)}) collective-permute-start(bf16[256,512]{1,0:T(8,128)(2,1)S(1)} %pad_maximum_fusion), channel_id=1, source_target_pairs={{0,248},{4,252},{8,0},{12,4},{16,8},{20,12},{24,16},{28,20},{32,24... | collective-permute-start | bytes 786440 | tf_op jit(solution)/shard_map/ppermute | solution.py:336
  18.8 5.0 %collective-permute-start.7 = (bf16[256,512]{1,0:T(8,128)(2,1)S(1)}, bf16[256,512]{1,0:T(8,128)(2,1)S(1)}, u32[]{:S(2)}, u32[]{:S(2)}) collective-permute-start(bf16[256,512]{1,0:T(8,128)(2,1)S(1)} %pad_maximum_fusion), channel_id=1, source_target_pairs={{0,240},{4,244},{8,248},{12,252},{16,0},{20,4},{24,8},{28,12},{32,... | collective-permute-start | bytes 786440 | tf_op jit(solution)/shard_map/ppermute | solution.py:336
  23.8 1.6 copy-done.1
  25.4 43.0 %attend_near.5.refs_0_.refs_1_ = bf16[256,512]{1,0:T(8,128)(2,1)S(1)} custom-call(f32[4]{0:T(128)S(1)} %copy-done.7, s32[4]{0:T(128)S(1)} %pad_add_fusion.facts_ref, bf16[128,512]{1,0:T(8,128)(2,1)S(1)} %prepare_queries.1.refs_0_, bf16[128,512]{1,0:T(8,128)(2,1)S(1)} %collective-permute-done.refs_1_, ...), custom_call_target="tpu_custom_call" | custom-call | flops 1073741824 | bytes 4194304 | tf_op jit(solution)/shard_map/attend_near/pallas_call | solution.py:294
  68.4 4.3 %attend_near.6 = bf16[256,512]{1,0:T(8,128)(2,1)S(1)} custom-call(f32[4]{0:T(128)S(1)} %copy-done.7, s32[4]{0:T(128)S(1)} %pad_add_fusion.1.facts_ref, bf16[256,512]{1,0:T(8,128)(2,1)S(1)} %collective-permute-done.1.refs_0_, bf16[4,2048,128]{2,1,0:T(8,128)(2,1)S(1)} %get-tuple-element.19.refs_2_.refs_1_, bf16[4,2048,128]{2,1,0:T(8,128)(2,1)S(1)} %copy-done.1), custom_call_target="tpu_custom_call" | custom-call | flops 1073741824 | bytes 4194304 | tf_op jit(solution)/shard_map/attend_near/pallas_call | solution.py:294
  72.7 4.5 %attend_near.7 = bf16[256,512]{1,0:T(8,128)(2,1)S(1)} custom-call(f32[4]{0:T(128)S(1)} %copy-done.7, s32[4]{0:T(128)S(1)} %pad_add_fusion.2.facts_ref, bf16[256,512]{1,0:T(8,128)(2,1)S(1)} %collective-permute-done.3.refs_0_, bf16[4,2048,128]{2,1,0:T(8,128)(2,1)S(1)} %get-tuple-element.19.refs_2_.refs_1_, bf16[4,2048,128]{2,1,0:T(8,128)(2,1)S(1)} %copy-done.1), custom_call_target="tpu_custom_call" | custom-call | flops 1073741824 | bytes 4194304 | tf_op jit(solution)/shard_map/attend_near/pallas_call | solution.py:294
  77.2 4.4 %attend_near.8 = bf16[256,512]{1,0:T(8,128)(2,1)S(1)} custom-call(f32[4]{0:T(128)S(1)} %copy-done.7, s32[4]{0:T(128)S(1)} %pad_add_fusion.3.facts_ref, bf16[256,512]{1,0:T(8,128)(2,1)S(1)} %collective-permute-done.5.refs_0_, bf16[4,2048,128]{2,1,0:T(8,128)(2,1)S(1)} %get-tuple-element.19.refs_2_.refs_1_, bf16[4,2048,128]{2,1,0:T(8,128)(2,1)S(1)} %copy-done.1), custom_call_target="tpu_custom_call" | custom-call | flops 1073741824 | bytes 4194304 | tf_op jit(solution)/shard_map/attend_near/pallas_call | solution.py:294
  81.6 4.4 %attend_near.9 = bf16[256,512]{1,0:T(8,128)(2,1)S(1)} custom-call(f32[4]{0:T(128)S(1)} %copy-done.7, s32[4]{0:T(128)S(1)} %pad_add_fusion.4.facts_ref, bf16[256,512]{1,0:T(8,128)(2,1)S(1)} %collective-permute-done.7.refs_0_, bf16[4,2048,128]{2,1,0:T(8,128)(2,1)S(1)} %get-tuple-element.19.refs_2_.refs_1_, bf16[4,2048,128]{2,1,0:T(8,128)(2,1)S(1)} %copy-done.1), custom_call_target="tpu_custom_call" | custom-call | flops 1073741824 | bytes 4194304 | tf_op jit(solution)/shard_map/attend_near/pallas_call | solution.py:294
  86.2 4.9 %collective-permute-start.6 = (bf16[256,512]{1,0:T(8,128)(2,1)S(1)}, bf16[256,512]{1,0:T(8,128)(2,1)S(1)}, u32[]{:S(2)}, u32[]{:S(2)}) collective-permute-start(bf16[256,512]{1,0:T(8,128)(2,1)S(1)} %attend_near.8), channel_id=1, source_target_pairs={{0,240},{4,244},{8,248},{12,252},{16,0},{20,4},{24,8},{28,12},{32,... | collective-permute-start | bytes 786440 | tf_op jit(solution)/shard_map/ppermute | solution.py:336
  91.1 4.1 %collective-permute-start.2 = (bf16[256,512]{1,0:T(8,128)(2,1)S(1)}, bf16[256,512]{1,0:T(8,128)(2,1)S(1)}, u32[]{:S(2)}, u32[]{:S(2)}) collective-permute-start(bf16[256,512]{1,0:T(8,128)(2,1)S(1)} %attend_near.6), channel_id=1, source_target_pairs={{0,248},{4,252},{8,0},{12,4},{16,8},{20,12},{24,16},{28,20},{32,24... | collective-permute-start | bytes 786440 | tf_op jit(solution)/shard_map/ppermute | solution.py:336
  95.3 3.6 %collective-permute-done.8.refs_4_.refs_5_ = bf16[256,512]{1,0:T(8,128)(2,1)S(1)} collective-permute-done((bf16[256,512]{1,0:T(8,128)(2,1)S(1)}, bf16[256,512]{1,0:T(8,128)(2,1)S(1)}, u32[]{:S(2)}, u32[]{:S(2)}) %collective-permute-start.8) | collective-permute-done | bytes 262176 | tf_op jit(solution)/shard_map/ppermute | solution.py:336
  98.9 72.2 %collective-permute-done.6.refs_3_.refs_4_ = bf16[256,512]{1,0:T(8,128)(2,1)S(1)} collective-permute-done((bf16[256,512]{1,0:T(8,128)(2,1)S(1)}, bf16[256,512]{1,0:T(8,128)(2,1)S(1)}, u32[]{:S(2)}, u32[]{:S(2)}) %collective-permute-start.6) | collective-permute-done | bytes 262176 | tf_op jit(solution)/shard_map/ppermute | solution.py:336
  171.1 2.7 %collective-permute-done.2.refs_1_.refs_2_ = bf16[256,512]{1,0:T(8,128)(2,1)S(1)} collective-permute-done((bf16[256,512]{1,0:T(8,128)(2,1)S(1)}, bf16[256,512]{1,0:T(8,128)(2,1)S(1)}, u32[]{:S(2)}, u32[]{:S(2)}) %collective-permute-start.2) | collective-permute-done | bytes 262176 | tf_op jit(solution)/shard_map/ppermute | solution.py:336
  173.8 1.0 merge_other.1
  175.0 5.0 %collective-permute-done.9.refs_0_ = bf16[128,512]{1,0:T(8,128)(2,1)S(1)} collective-permute-done((bf16[128,512]{1,0:T(8,128)(2,1)S(1)}, bf16[128,512]{1,0:T(8,128)(2,1)S(1)}, u32[]{:S(2)}, u32[]{:S(2)}) %collective-permute-start.9) | collective-permute-done | bytes 131104 | tf_op jit(solution)/shard_map/ppermute | solution.py:340
  179.9 1.3 merge.1
  181.3 1.4 collective-permute-done.10
  182.7 1.8 collective-permute-start.11
  184.6 4.6 %collective-permute-done.11 = bf16[128,384]{1,0:T(8,128)(2,1)S(1)} collective-permute-done((bf16[128,384]{1,0:T(8,128)(2,1)S(1)}, bf16[128,384]{1,0:T(8,128)(2,1)S(1)}, u32[]{:S(2)}, u32[]{:S(2)}) %collective-permute-start.11) | collective-permute-done | bytes 98336 | tf_op jit(solution)/shard_map/ppermute | solution.py:340
  189.2 0.7 fusion
  (31 shorter events, 0.9 us)
Async XLA Ops:
  0.0 0.9 copy-start.5
  0.9 0.9 copy-start.6
  1.8 0.7 copy-start.8
  2.4 0.7 copy-start.9
  3.1 0.7 copy-start.10
  4.4 8.3 %collective-permute-start = (bf16[128,512]{1,0:T(8,128)(2,1)S(1)}, bf16[128,512]{1,0:T(8,128)(2,1)S(1)}, u32[]{:S(2)}, u32[]{:S(2)}) collective-permute-start(bf16[128,512]{1,0:T(8,128)(2,1)S(1)} %prepare_queries.1.refs_0_), channel_id=1, source_target_pairs={{0,4},{4,0},{8,12},{12,8},{16,20},{20,16},{24,28},{28,24},{32,36},... | collective-permute-start | bytes 393224 | tf_op jit(solution)/shard_map/ppermute | solution.py:340
  6.2 1.4 copy-start.2
  7.6 1.4 copy-start.3
  9.0 14.8 %copy-start.7 = (f32[4]{0:T(128)S(1)}, f32[4]{0:T(128)}, u32[]{:S(2)}) copy-start(f32[4]{0:T(128)} %slopes_ref.9) | copy-start | bytes 52
  11.2 1.3 copy-start
  12.7 55.7 %collective-permute-start.1 = (bf16[256,512]{1,0:T(8,128)(2,1)S(1)}, bf16[256,512]{1,0:T(8,128)(2,1)S(1)}, u32[]{:S(2)}, u32[]{:S(2)}) collective-permute-start(bf16[256,512]{1,0:T(8,128)(2,1)S(1)} %pad_maximum_fusion), channel_id=1, source_target_pairs={{0,8},{4,12},{8,16},{12,20},{16,24},{20,28},{24,32},{28,36},{32,40... | collective-permute-start | bytes 786440 | tf_op jit(solution)/shard_map/ppermute | solution.py:336
  14.8 57.9 %collective-permute-start.3 = (bf16[256,512]{1,0:T(8,128)(2,1)S(1)}, bf16[256,512]{1,0:T(8,128)(2,1)S(1)}, u32[]{:S(2)}, u32[]{:S(2)}) collective-permute-start(bf16[256,512]{1,0:T(8,128)(2,1)S(1)} %pad_maximum_fusion), channel_id=1, source_target_pairs={{0,248},{4,252},{8,0},{12,4},{16,8},{20,12},{24,16},{28,20},{32,24... | collective-permute-start | bytes 786440 | tf_op jit(solution)/shard_map/ppermute | solution.py:336
  18.8 58.4 %collective-permute-start.5 = (bf16[256,512]{1,0:T(8,128)(2,1)S(1)}, bf16[256,512]{1,0:T(8,128)(2,1)S(1)}, u32[]{:S(2)}, u32[]{:S(2)}) collective-permute-start(bf16[256,512]{1,0:T(8,128)(2,1)S(1)} %pad_maximum_fusion), channel_id=1, source_target_pairs={{0,16},{4,20},{8,24},{12,28},{16,32},{20,36},{24,40},{28,44},{32,4... | collective-permute-start | bytes 786440 | tf_op jit(solution)/shard_map/ppermute | solution.py:336
  18.8 62.8 %collective-permute-start.7 = (bf16[256,512]{1,0:T(8,128)(2,1)S(1)}, bf16[256,512]{1,0:T(8,128)(2,1)S(1)}, u32[]{:S(2)}, u32[]{:S(2)}) collective-permute-start(bf16[256,512]{1,0:T(8,128)(2,1)S(1)} %pad_maximum_fusion), channel_id=1, source_target_pairs={{0,240},{4,244},{8,248},{12,252},{16,0},{20,4},{24,8},{28,12},{32,... | collective-permute-start | bytes 786440 | tf_op jit(solution)/shard_map/ppermute | solution.py:336
  23.8 1.6 copy-start.1
  86.0 93.9 %copy-start.4 = (bf16[384,1536]{1,0:T(8,128)(2,1)S(1)}, bf16[384,1536]{1,0:T(8,128)(2,1)}, u32[]{:S(2)}) copy-start(bf16[384,1536]{1,0:T(8,128)(2,1)} %refs_6_.1) | copy-start | bytes 3538948
  86.0 12.9 %collective-permute-start.8 = (bf16[256,512]{1,0:T(8,128)(2,1)S(1)}, bf16[256,512]{1,0:T(8,128)(2,1)S(1)}, u32[]{:S(2)}, u32[]{:S(2)}) collective-permute-start(bf16[256,512]{1,0:T(8,128)(2,1)S(1)} %attend_near.9), channel_id=1, source_target_pairs={{0,16},{4,20},{8,24},{12,28},{16,32},{20,36},{24,40},{28,44},{32,4... | collective-permute-start | bytes 786440 | tf_op jit(solution)/shard_map/ppermute | solution.py:336
  86.2 84.9 %collective-permute-start.6 = (bf16[256,512]{1,0:T(8,128)(2,1)S(1)}, bf16[256,512]{1,0:T(8,128)(2,1)S(1)}, u32[]{:S(2)}, u32[]{:S(2)}) collective-permute-start(bf16[256,512]{1,0:T(8,128)(2,1)S(1)} %attend_near.8), channel_id=1, source_target_pairs={{0,240},{4,244},{8,248},{12,252},{16,0},{20,4},{24,8},{28,12},{32,... | collective-permute-start | bytes 786440 | tf_op jit(solution)/shard_map/ppermute | solution.py:336
  91.1 80.0 %collective-permute-start.4 = (bf16[256,512]{1,0:T(8,128)(2,1)S(1)}, bf16[256,512]{1,0:T(8,128)(2,1)S(1)}, u32[]{:S(2)}, u32[]{:S(2)}) collective-permute-start(bf16[256,512]{1,0:T(8,128)(2,1)S(1)} %attend_near.7), channel_id=1, source_target_pairs={{0,8},{4,12},{8,16},{12,20},{16,24},{20,28},{24,32},{28,36},{32,40... | collective-permute-start | bytes 786440 | tf_op jit(solution)/shard_map/ppermute | solution.py:336
  91.1 82.7 %collective-permute-start.2 = (bf16[256,512]{1,0:T(8,128)(2,1)S(1)}, bf16[256,512]{1,0:T(8,128)(2,1)S(1)}, u32[]{:S(2)}, u32[]{:S(2)}) collective-permute-start(bf16[256,512]{1,0:T(8,128)(2,1)S(1)} %attend_near.6), channel_id=1, source_target_pairs={{0,248},{4,252},{8,0},{12,4},{16,8},{20,12},{24,16},{28,20},{32,24... | collective-permute-start | bytes 786440 | tf_op jit(solution)/shard_map/ppermute | solution.py:336
  174.8 5.1 %collective-permute-start.9 = (bf16[128,512]{1,0:T(8,128)(2,1)S(1)}, bf16[128,512]{1,0:T(8,128)(2,1)S(1)}, u32[]{:S(2)}, u32[]{:S(2)}) collective-permute-start(bf16[128,512]{1,0:T(8,128)(2,1)S(1)} %merge_other.1), channel_id=1, source_target_pairs={{0,4},{4,0},{8,12},{12,8},{16,20},{20,16},{24,28},{28,24},{32,36},... | collective-permute-start | bytes 393224 | tf_op jit(solution)/shard_map/ppermute | solution.py:340
  181.2 1.5 collective-permute-start.10
  182.7 6.4 %collective-permute-start.11 = (bf16[128,384]{1,0:T(8,128)(2,1)S(1)}, bf16[128,384]{1,0:T(8,128)(2,1)S(1)}, u32[]{:S(2)}, u32[]{:S(2)}) collective-permute-start(bf16[128,384]{1,0:T(8,128)(2,1)S(1)} %fusion.1), channel_id=1, source_target_pairs={{0,2},{1,3},{2,0},{3,1},{4,6},{5,7},{6,4},{7,5},{8,10},{9,11},{10,... | collective-permute-start | bytes 294920 | tf_op jit(solution)/shard_map/ppermute | solution.py:340

commit v3 on v2

v3 whole, which is shorter than its diff:
```python
import functools
import math

import jax
import jax.numpy as jnp
from jax import lax
from jax.experimental import pallas as pl
from jax.experimental.pallas import tpu as pltpu
from jax.sharding import PartitionSpec as P

HEAD_DIM = 96
RADIUS = 7812
SHIFT = 64
LANES = 128
LOG2E = math.log2(math.e)
SCALE2 = LOG2E / math.sqrt(HEAD_DIM)
FAR = 1e30
EMPTY = -16384.0
SUM_LO, SUM_HI = 2.0**-60, 2.0**100
TILE = 512
ORDER = (2, 3, 0, 1)
QUERY_VMEM = 4 * 2**20
EXTRA = 16

SMEM = pl.BlockSpec(memory_space=pltpu.SMEM)
VMEM = pl.BlockSpec(memory_space=pltpu.VMEM)
HBM = pl.BlockSpec(memory_space=pltpu.HBM)


def query_kernel(base_ref, *refs):
    sources, out_ref, copies, sems = refs[:5], refs[5], refs[6:11], refs[11]
    moves = [pltpu.make_async_copy(a, b, sems.at[i]) for i, (a, b) in enumerate(zip(sources, copies))]
    for move in moves:
        move.start()
    for move in moves:
        move.wait()
    types_ref, promoters_ref, offsets_ref, queries_ref, embed_ref = copies
    rows, width = queries_ref.shape
    kinds = embed_ref.shape[0]
    one_hot = (lax.broadcasted_iota(jnp.int32, (kinds, rows), 0) == types_ref[...]).astype(jnp.float32)
    embedded = jnp.dot(one_hot.T.astype(jnp.bfloat16), embed_ref[...], preferred_element_type=jnp.float32)
    query = queries_ref[...].astype(jnp.float32) + embedded
    out_ref[:width, :] = query.T.astype(jnp.bfloat16)
    place = promoters_ref[...] + offsets_ref[...] - base_ref[0] + SHIFT
    coarse = lax.shift_right_arithmetic(place, 4) * 16
    line = lax.broadcasted_iota(jnp.int32, (EXTRA, rows), 0)
    extra = jnp.where(line == 0, coarse, jnp.where(line == 1, place - coarse, 0))
    out_ref[width:, :] = extra.astype(jnp.float32).astype(jnp.bfloat16)


def bins_kernel(values_ref, out_ref):
    groups, _, bins = out_ref.shape
    values = values_ref[...].T
    for g in range(groups):
        out_ref[g, :HEAD_DIM, :] = values[g * HEAD_DIM : (g + 1) * HEAD_DIM]
        out_ref[g, HEAD_DIM:, :] = jnp.ones((EXTRA, bins), jnp.bfloat16)


def block_facts(extra, strides, stride, bins, ok):
    extra = extra.astype(jnp.float32)
    centre = extra[0:1] + extra[1:2] - (stride * bins + SHIFT).astype(jnp.float32)
    before, after = -centre, centre - float(bins - 1)
    if strides == (0,):
        base = jnp.zeros_like(centre)
    elif min(strides) > 0:
        base = before
    elif max(strides) < 0:
        base = after
    else:
        base = jnp.maximum(before, after)
    alive = jnp.where(jnp.maximum(before, after) <= RADIUS, 1.0, 0.0) * jnp.where(ok, 1.0, 0.0)
    return centre, base, alive


def tile_needs(strides, bins, start, size):
    bends, ends = min(strides) <= 0 <= max(strides), False
    for stride in strides:
        low, high = -SHIFT - stride * bins, bins - 1 + SHIFT - stride * bins
        if max(-high, low - (bins - 1)) > RADIUS:
            continue
        if stride >= 0:
            bends |= high > start
            ends |= start + size - 1 - low > RADIUS
        if stride <= 0:
            bends |= low < start + size - 1
            ends |= high - start > RADIUS
    return bends, ends


def attend_rows(blocks, strides, oks, slopes, query_refs, keys_ref, values_ref, out_refs, acc_ref):
    bins, width = keys_ref.shape
    groups = values_ref.shape[0]
    rows = query_refs[0].shape[1]
    n = len(query_refs)
    parts = [slice(i * rows, (i + 1) * rows) for i in range(n)]
    facts = [block_facts(ref[width:, :], *each, bins, ok) for ref, *each, ok in zip(query_refs, blocks, strides, oks)]
    centre, base, alive = (jnp.concatenate([fact[k] for fact in facts], axis=1) for k in range(3))
    alive = alive > 0.0
    windows, queries = [], []
    for g in range(groups):
        low, high = g * HEAD_DIM, (g + 1) * HEAD_DIM
        first, last = low // LANES * LANES, -(-high // LANES) * LANES
        query = jnp.concatenate([ref[low:high, :] for ref in query_refs], axis=1)
        pads = [jnp.zeros((size, n * rows), jnp.bfloat16) for size in (low - first, last - high)]
        pieces = [piece for piece in (pads[0], query, pads[1]) if piece.shape[0]]
        windows.append(slice(first, last))
        queries.append(jnp.concatenate(pieces, axis=0))

    def products(g, start, size):
        return jnp.dot(keys_ref[pl.ds(start, size), windows[g]], queries[g], preferred_element_type=jnp.float32)

    def positions(start, size):
        return (start + lax.broadcasted_iota(jnp.int32, (size, 1), 0)).astype(jnp.float32)

    line = lax.broadcasted_iota(jnp.int32, (EXTRA, n * rows), 0)

    def finish(g, acc, shift, extra):
        exponent = shift - slopes[g] * base
        coarse = jnp.where(alive, jnp.round(exponent * 0.0625) * 16.0, EMPTY)
        factor = jnp.where(alive, jnp.exp2(exponent - coarse), 0.0)
        scaled = jnp.where(alive, acc * factor, 0.0)
        total = scaled[HEAD_DIM : HEAD_DIM + 1]
        high = total.astype(jnp.bfloat16).astype(jnp.float32)
        for part, ref in zip(parts, out_refs):
            ref[g * HEAD_DIM : (g + 1) * HEAD_DIM, :] = scaled[:HEAD_DIM, part].astype(jnp.bfloat16)
        for k, row in enumerate((high, total - high, coarse)):
            extra = jnp.where(line == k * groups + g, row, extra)
        return extra

    def finished(extra):
        for part, ref in zip(parts, out_refs):
            ref[width:, :] = extra[:, part].astype(jnp.bfloat16)

    accs = [None] * groups
    for start in range(0, bins, TILE):
        position = positions(start, TILE)
        shapes = []
        for block, (middle, origin, _) in zip(blocks, facts):
            bends, ends = tile_needs(block, bins, start, TILE)
            if bends:
                distance = jnp.abs(position - middle) - origin
            else:
                distance = position if min(block) > 0 else float(bins - 1) - position
            shapes.append((distance, jnp.abs(position - middle) <= RADIUS if ends else None))
        weights = []
        for g in range(groups):
            raw = products(g, start, TILE)
            pieces = []
            for part, (distance, usable) in zip(parts, shapes):
                weight = jnp.exp2(raw[:, part] * SCALE2 - slopes[g] * distance)
                weight = weight if usable is None else jnp.where(usable, weight, 0.0)
                pieces.append(weight.astype(jnp.bfloat16))
            weights.append(jnp.concatenate(pieces, axis=1))
        for g in range(groups):
            gained = jnp.dot(values_ref[g, :, start : start + TILE], weights[g], preferred_element_type=jnp.float32)
            accs[g] = gained if accs[g] is None else accs[g] + gained
    wrong = jnp.zeros((1, n * rows), jnp.float32)
    extra = jnp.zeros((EXTRA, n * rows), jnp.float32)
    for g in range(groups):
        total = accs[g][HEAD_DIM : HEAD_DIM + 1]
        wrong = jnp.where((total >= SUM_LO) & (total <= SUM_HI), wrong, 1.0)
        extra = finish(g, accs[g], 0.0, extra)
    finished(extra)

    @pl.when(jnp.max(jnp.where(alive, wrong, 0.0)) > 0.0)
    def _():
        extra = jnp.zeros((EXTRA, n * rows), jnp.float32)
        for g in range(groups):

            def logs(k):
                start = pl.multiple_of(k * LANES, LANES)
                distance = jnp.abs(positions(start, LANES) - centre)
                exponent = products(g, start, LANES) * SCALE2 - slopes[g] * (distance - base)
                return start, jnp.where(distance <= RADIUS, exponent, -FAR)

            def largest(k, so_far):
                return jnp.maximum(so_far, jnp.max(logs(k)[1], axis=0, keepdims=True))

            shift = lax.fori_loop(0, bins // LANES, largest, jnp.full((1, n * rows), -FAR, jnp.float32))
            acc_ref[...] = jnp.zeros_like(acc_ref)

            @pl.loop(0, bins // LANES)
            def _(k):
                start, exponent = logs(k)
                weights = jnp.exp2(exponent - shift).astype(jnp.bfloat16)
                acc_ref[...] += jnp.dot(values_ref[g, :, pl.ds(start, LANES)], weights, preferred_element_type=jnp.float32)

            extra = finish(g, acc_ref[...], shift, extra)
        finished(extra)


def near_kernel(shifts, seq_count, slopes_ref, position_ref, *refs):
    query_refs, (keys_ref, values_ref, out_ref, acc_ref) = refs[:-4], refs[-4:]
    if len(query_refs) == 1:
        query_refs = [query_refs[0].at[i] for i in range(len(shifts))]
    position = position_ref[0]
    odd = position & 1
    blocks, strides, oks = [], [], []
    for shift, same in shifts:
        block = (2 * shift,) if same else (2 * shift - 1, 2 * shift + 1)
        stride = jnp.int32(2 * shift) if same else 2 * shift + 2 * odd - 1
        blocks.append(block)
        strides.append(stride)
        oks.append((position - stride >= 0) & (position - stride < seq_count))
    attend_rows(
        blocks,
        strides,
        oks,
        [slopes_ref[g] * LOG2E for g in range(values_ref.shape[0])],
        query_refs,
        keys_ref,
        values_ref,
        [out_ref.at[i] for i in range(len(shifts))],
        acc_ref,
    )


def combined(groups, refs):
    width = groups * HEAD_DIM
    extras = [ref[width:, :].astype(jnp.float32) for ref in refs]
    found = []
    for g in range(groups):
        scales = [extra[2 * groups + g : 2 * groups + g + 1] for extra in extras]
        top = functools.reduce(jnp.maximum, scales)
        acc, total = 0.0, 0.0
        for ref, extra, scale in zip(refs, extras, scales):
            factor = jnp.exp2(scale - top)
            acc += ref[g * HEAD_DIM : (g + 1) * HEAD_DIM, :].astype(jnp.float32) * factor
            total += (extra[g : g + 1] + extra[groups + g : groups + g + 1]) * factor
        found.append((acc, total, top))
    return found


def other_kernel(groups, *refs):
    part_refs, out_ref = refs[:-1], refs[-1]
    width = groups * HEAD_DIM
    line = lax.broadcasted_iota(jnp.int32, (EXTRA, out_ref.shape[1]), 0)
    extra = jnp.zeros(line.shape, jnp.float32)
    for g, (acc, total, top) in enumerate(combined(groups, [ref.at[1] for ref in part_refs])):
        high = total.astype(jnp.bfloat16).astype(jnp.float32)
        for k, row in enumerate((high, total - high, top)):
            extra = jnp.where(line == k * groups + g, row, extra)
        out_ref[g * HEAD_DIM : (g + 1) * HEAD_DIM, :] = acc.astype(jnp.bfloat16)
    out_ref[width:, :] = extra.astype(jnp.bfloat16)


def merge_kernel(groups, place_ref, theirs_ref, *refs):
    part_refs, (w_ref, keep_ref, send_ref) = refs[:-3], refs[-3:]
    shares = combined(groups, [theirs_ref] + [ref.at[0] for ref in part_refs])
    pooled = jnp.concatenate([acc / total for acc, total, _ in shares], axis=0).T.astype(jnp.bfloat16)
    width = w_ref.shape[1] // 4
    core, high = place_ref[0] & 1, place_ref[0] >> 1
    for k in range(2):
        row = (high if k == 0 else 1 - high) * 2
        for ref, lane in ((send_ref, 1 - core), (keep_ref, core)):
            start = pl.multiple_of((row + lane) * width, LANES)
            ref[k] = jnp.dot(pooled, w_ref[:, pl.ds(start, width)], preferred_element_type=jnp.float32).astype(ref.dtype)


def prepare_queries(queries, cell_types, promoters, offsets, cell_embed, base):
    rows, width = queries.shape
    sources = [cell_types[None, :], promoters[None, :], offsets[None, :], queries, cell_embed]
    return pl.pallas_call(
        query_kernel,
        in_specs=[SMEM] + [HBM] * 5,
        out_specs=VMEM,
        out_shape=jax.ShapeDtypeStruct((width + EXTRA, rows), jnp.bfloat16),
        scratch_shapes=[pltpu.VMEM(a.shape, a.dtype) for a in sources] + [pltpu.SemaphoreType.DMA((5,))],
        compiler_params=pltpu.CompilerParams(vmem_limit_bytes=QUERY_VMEM),
        name="prepare_queries",
    )(base[None], *sources)


def prepare_bins(values, groups):
    bins = values.shape[0]
    return pl.pallas_call(
        bins_kernel,
        in_specs=[VMEM],
        out_specs=VMEM,
        out_shape=jax.ShapeDtypeStruct((groups, HEAD_DIM + EXTRA, bins), jnp.bfloat16),
        compiler_params=pltpu.CompilerParams(vmem_limit_bytes=16 * 2**20),
        cost_estimate=pl.CostEstimate(flops=0, bytes_accessed=4 * 2**20, transcendentals=0),
        name="prepare_bins",
    )(values)


def attend_near(shifts, seq_count, slopes, position, queries, keys, values):
    groups, depth, bins = values.shape
    n = len(shifts)
    height, rows = queries[0].shape[-2:]
    return pl.pallas_call(
        functools.partial(near_kernel, shifts, seq_count),
        in_specs=[SMEM, SMEM] + [VMEM] * (len(queries) + 2),
        out_specs=VMEM,
        out_shape=jax.ShapeDtypeStruct((n, height, rows), jnp.bfloat16),
        scratch_shapes=[pltpu.VMEM((depth, n * rows), jnp.float32)],
        compiler_params=pltpu.CompilerParams(vmem_limit_bytes=24 * 2**20),
        cost_estimate=pl.CostEstimate(
            flops=4 * n * rows * bins * groups * LANES, bytes_accessed=4 * 2**20, transcendentals=n * rows * bins * groups
        ),
        name="attend_near",
    )(slopes, position[None], *queries, keys, values)


def merge_other(parts, groups):
    return pl.pallas_call(
        functools.partial(other_kernel, groups),
        in_specs=[VMEM] * len(parts),
        out_specs=VMEM,
        out_shape=jax.ShapeDtypeStruct(parts[0].shape[1:], jnp.bfloat16),
        compiler_params=pltpu.CompilerParams(vmem_limit_bytes=8 * 2**20),
        name="merge_other",
    )(*parts)


def merge(place, theirs, parts, w_out, groups):
    rows = theirs.shape[1]
    width = w_out.shape[1] // 4
    return pl.pallas_call(
        functools.partial(merge_kernel, groups),
        in_specs=[SMEM] + [VMEM] * (len(parts) + 2),
        out_specs=[VMEM] * 2,
        out_shape=[
            jax.ShapeDtypeStruct((2, rows, width), jnp.float32),
            jax.ShapeDtypeStruct((2, rows, width), jnp.bfloat16),
        ],
        compiler_params=pltpu.CompilerParams(vmem_limit_bytes=12 * 2**20),
        name="merge",
    )(place[None], theirs, *parts, w_out)


def rotated(value, steps):
    count = lax.axis_size("seq")
    return lax.ppermute(value, "seq", [(i, (i + steps) % count) for i in range(count)])


def swapped(value, axis, bit):
    return lax.ppermute(value, axis, [(i, i ^ bit) for i in range(lax.axis_size(axis))])


def local(queries, cell_types, promoters, offsets, cell_embed, bin_keys, bin_values, slopes, w_out):
    seq_count = lax.axis_size("seq")
    position = lax.axis_index("seq")
    place = lax.axis_index("head")
    bins = bin_keys.shape[0]
    groups = slopes.shape[0]

    mine = prepare_queries(queries, cell_types, promoters, offsets, cell_embed, position * bins)
    other = swapped(mine, "seq", 1)
    values = prepare_bins(bin_values, groups)
    other, values = lax.optimization_barrier((other, values))
    both = jnp.stack([mine, other])
    shifts = [2, -2, 1, -1]
    arrived = [rotated(both, 2 * shift) for shift in shifts]
    part = attend_near(((0, True), (0, False)), seq_count, slopes, position, [mine, other], bin_keys, values)
    parts = [part]
    for k in ORDER:
        shift = shifts[k]
        query = arrived[k]
        if k == ORDER[0]:
            query, _ = lax.optimization_barrier((query, part))
        share = attend_near(((shift, True), (shift, False)), seq_count, slopes, position, [query], bin_keys, values)
        parts.append(rotated(share, -2 * shift))
    theirs = swapped(merge_other(parts, groups), "seq", 1)
    keep, send = merge(place, theirs, parts, w_out, groups)
    got = swapped(send, "head", 1)
    rest = (keep[1] + got[1].astype(jnp.float32)).astype(jnp.bfloat16)
    last = swapped(rest, "head", 2)
    return (keep[0] + got[0].astype(jnp.float32) + last.astype(jnp.float32)).astype(jnp.bfloat16)


def solution(mesh):
    return jax.shard_map(
        local,
        mesh=mesh,
        in_specs=(
            P("seq", "head"),
            P("seq"),
            P("seq"),
            P("seq"),
            P(None, "head"),
            P("seq", "head"),
            P("seq", "head"),
            P("head"),
            P("head", None),
        ),
        out_specs=P("seq", "head"),
        check_vma=False,
    )
```

time: 193 us -> 181 us (0.938)
  the two profiles are of different devices: /device:TPU:2 before, /device:TPU:168 now
where the time goes in v3:
time: 181 us; the launch traced here: 180 us
  Pallas kernels  112 us (62%)
  starting transfers between devices  41 us (23%)
  waiting for transfers between devices  20.4 us (11%)
  local copies, waits for them, and re-layouts  5.17 us (3%)
    pallas_call x5, Pallas kernels, attend_near(): pl.pallas_call(functools.partial(near_kernel, shifts, seq_count), in_spec...  110 us
    ppermute x8, starting transfers between devices, rotated(): lax.ppermute(value, 'seq', [(i, (i + steps) % count) for i in range(count)])  40.2 us
    ppermute x4, waiting for transfers between devices, swapped(): lax.ppermute(value, axis, [(i, i ^ bit) for i in range(lax.axis_size(axis...  14.7 us
    ppermute x8, waiting for transfers between devices, rotated(): lax.ppermute(value, 'seq', [(i, (i + steps) % count) for i in range(count)])  5.73 us
    unnamed x18, local copies, waits for them, and re-layouts  5.17 us
  transfers between devices with their start and end apart: 12, of which 5 were waited for; matrix products, arithmetic and copies ran while one was open for 0% of the time, Pallas kernels for 62%

profile of v3, /device:TPU:168, one launch (start us, length us, event | category | flops | bytes accessed | tf_op | source)
XLA Modules:
  0.0 179.6 jit_solution(5430197401451735087)
XLA Ops:
  0.0 0.9 copy-done.2
  0.9 0.9 copy-done.3
  1.8 0.7 copy-done.4
  2.4 0.7 copy-done.5
  3.1 0.7 copy-done.6
  3.8 0.6 prepare_queries.1.refs_0_
  4.4 0.5 collective-permute-start
  4.9 1.4 copy-done
  6.3 0.5 prepare_bins.1.refs_3_.refs_2_
  6.8 2.3 %collective-permute-done.refs_1_ = bf16[400,128]{1,0:T(8,128)(2,1)S(1)} collective-permute-done((bf16[400,128]{1,0:T(8,128)(2,1)S(1)}, bf16[400,128]{1,0:T(8,128)(2,1)S(1)}, u32[]{:S(2)}, u32[]{:S(2)}) %collective-permute-start) | collective-permute-done | bytes 102432 | tf_op jit(solution)/shard_map/ppermute | solution.py:338
  9.1 0.6 collective-permute-start.7
  9.8 2.4 %collective-permute-start.5 = (bf16[2,400,128]{2,1,0:T(8,128)(2,1)S(1)}, bf16[2,400,128]{2,1,0:T(8,128)(2,1)S(1)}, u32[]{:S(2)}, u32[]{:S(2)}) collective-permute-start(bf16[2,400,128]{2,1,0:T(8,128)(2,1)S(1)} %pad_maximum_fusion), channel_id=1, source_target_pairs={{0,16},{4,20},{8,24},{12,28},{16,32},{20,36},{24,40},{28,44},{32,4... | collective-permute-start | bytes 614408 | tf_op jit(solution)/shard_map/ppermute | solution.py:334
  12.1 1.0 collective-permute-start.3
  13.1 2.1 %collective-permute-start.1 = (bf16[2,400,128]{2,1,0:T(8,128)(2,1)S(1)}, bf16[2,400,128]{2,1,0:T(8,128)(2,1)S(1)}, u32[]{:S(2)}, u32[]{:S(2)}) collective-permute-start(bf16[2,400,128]{2,1,0:T(8,128)(2,1)S(1)} %pad_maximum_fusion), channel_id=1, source_target_pairs={{0,8},{4,12},{8,16},{12,20},{16,24},{20,28},{24,32},{28,36},{32,40... | collective-permute-start | bytes 614408 | tf_op jit(solution)/shard_map/ppermute | solution.py:334
  15.3 35.0 %attend_near.5.refs_0_ = bf16[2,400,128]{2,1,0:T(8,128)(2,1)S(1)} custom-call(f32[4]{0:T(128)S(1)} %copy-done.8, s32[1]{0:T(128)} %bitcast.1.position_ref, bf16[400,128]{1,0:T(8,128)(2,1)S(1)} %prepare_queries.1.refs_0_, bf16[400,128]{1,0:T(8,128)(2,1)S(1)} %collective-permute-done.refs_1_, bf16[2048,384]{1,0:T(8,128)(2,1)S(1)} %copy-done.7, ...), custom_call_target="tpu_custom_call" | custom-call | flops 1073741824 | bytes 4194304 | tf_op jit(solution)/shard_map/attend_near/pallas_call | solution.py:291
  50.3 2.8 %attend_near.9 = bf16[2,400,128]{2,1,0:T(8,128)(2,1)S(1)} custom-call(f32[4]{0:T(128)S(1)} %copy-done.8, s32[1]{0:T(128)} %bitcast.1.position_ref, bf16[2,400,128]{2,1,0:T(8,128)(2,1)S(1)} %collective-permute-done.7.refs_0_, bf16[2048,384]{1,0:T(8,128)(2,1)S(1)} %copy-done.7, bf16[4,112,2048]{2,1,0:T(8,128)(2,1)S(1)} %prepare_bins.1.refs_3_.refs_2_), custom_call_target="tpu_custom_call" | custom-call | flops 1073741824 | bytes 4194304 | tf_op jit(solution)/shard_map/attend_near/pallas_call | solution.py:291
  53.2 4.8 %collective-permute-start.8 = (bf16[2,400,128]{2,1,0:T(8,128)(2,1)S(1)}, bf16[2,400,128]{2,1,0:T(8,128)(2,1)S(1)}, u32[]{:S(2)}, u32[]{:S(2)}) collective-permute-start(bf16[2,400,128]{2,1,0:T(8,128)(2,1)S(1)} %attend_near.9), channel_id=1, source_target_pairs={{0,16},{4,20},{8,24},{12,28},{16,32},{20,36},{24,40},{28,44},{32,4... | collective-permute-start | bytes 614408 | tf_op jit(solution)/shard_map/ppermute | solution.py:334
  58.0 2.8 %attend_near.8 = bf16[2,400,128]{2,1,0:T(8,128)(2,1)S(1)} custom-call(f32[4]{0:T(128)S(1)} %copy-done.8, s32[1]{0:T(128)} %bitcast.1.position_ref, bf16[2,400,128]{2,1,0:T(8,128)(2,1)S(1)} %collective-permute-done.5.refs_0_, bf16[2048,384]{1,0:T(8,128)(2,1)S(1)} %copy-done.7, bf16[4,112,2048]{2,1,0:T(8,128)(2,1)S(1)} %prepare_bins.1.refs_3_.refs_2_), custom_call_target="tpu_custom_call" | custom-call | flops 1073741824 | bytes 4194304 | tf_op jit(solution)/shard_map/attend_near/pallas_call | solution.py:291
  60.8 0.1 collective-permute-start.6
  60.9 34.9 %attend_near.7 = bf16[2,400,128]{2,1,0:T(8,128)(2,1)S(1)} custom-call(f32[4]{0:T(128)S(1)} %copy-done.8, s32[1]{0:T(128)} %bitcast.1.position_ref, bf16[2,400,128]{2,1,0:T(8,128)(2,1)S(1)} %collective-permute-done.3.refs_0_, bf16[2048,384]{1,0:T(8,128)(2,1)S(1)} %copy-done.7, bf16[4,112,2048]{2,1,0:T(8,128)(2,1)S(1)} %prepare_bins.1.refs_3_.refs_2_), custom_call_target="tpu_custom_call" | custom-call | flops 1073741824 | bytes 4194304 | tf_op jit(solution)/shard_map/attend_near/pallas_call | solution.py:291
  95.8 29.0 %collective-permute-start.4 = (bf16[2,400,128]{2,1,0:T(8,128)(2,1)S(1)}, bf16[2,400,128]{2,1,0:T(8,128)(2,1)S(1)}, u32[]{:S(2)}, u32[]{:S(2)}) collective-permute-start(bf16[2,400,128]{2,1,0:T(8,128)(2,1)S(1)} %attend_near.7), channel_id=1, source_target_pairs={{0,8},{4,12},{8,16},{12,20},{16,24},{20,28},{24,32},{28,36},{32,40... | collective-permute-start | bytes 614408 | tf_op jit(solution)/shard_map/ppermute | solution.py:334
  124.9 34.8 %attend_near.6 = bf16[2,400,128]{2,1,0:T(8,128)(2,1)S(1)} custom-call(f32[4]{0:T(128)S(1)} %copy-done.8, s32[1]{0:T(128)} %bitcast.1.position_ref, bf16[2,400,128]{2,1,0:T(8,128)(2,1)S(1)} %collective-permute-done.1.refs_0_, bf16[2048,384]{1,0:T(8,128)(2,1)S(1)} %copy-done.7, bf16[4,112,2048]{2,1,0:T(8,128)(2,1)S(1)} %prepare_bins.1.refs_3_.refs_2_), custom_call_target="tpu_custom_call" | custom-call | flops 1073741824 | bytes 4194304 | tf_op jit(solution)/shard_map/attend_near/pallas_call | solution.py:291
  159.8 5.7 %collective-permute-done.2.refs_1_ = bf16[2,400,128]{2,1,0:T(8,128)(2,1)S(1)} collective-permute-done((bf16[2,400,128]{2,1,0:T(8,128)(2,1)S(1)}, bf16[2,400,128]{2,1,0:T(8,128)(2,1)S(1)}, u32[]{:S(2)}, u32[]{:S(2)}) %collective-permute-start.2) | collective-permute-done | bytes 204832 | tf_op jit(solution)/shard_map/ppermute | solution.py:334
  165.5 0.1 merge_other.1
  165.7 0.1 collective-permute-start.9
  165.8 4.6 %collective-permute-done.9.theirs_ref = bf16[400,128]{1,0:T(8,128)(2,1)S(1)} collective-permute-done((bf16[400,128]{1,0:T(8,128)(2,1)S(1)}, bf16[400,128]{1,0:T(8,128)(2,1)S(1)}, u32[]{:S(2)}, u32[]{:S(2)}) %collective-permute-start.9) | collective-permute-done | bytes 102432 | tf_op jit(solution)/shard_map/ppermute | solution.py:338
  170.4 0.6 merge.1
  171.0 0.1 collective-permute-start.10
  171.1 1.4 collective-permute-done.10
  172.5 0.1 collective-permute-start.11
  172.6 6.3 %collective-permute-done.11 = bf16[128,384]{1,0:T(8,128)(2,1)S(1)} collective-permute-done((bf16[128,384]{1,0:T(8,128)(2,1)S(1)}, bf16[128,384]{1,0:T(8,128)(2,1)S(1)}, u32[]{:S(2)}, u32[]{:S(2)}) %collective-permute-start.11) | collective-permute-done | bytes 98336 | tf_op jit(solution)/shard_map/ppermute | solution.py:338
  179.0 0.7 fusion
  (22 shorter events, 0.2 us)
Async XLA Ops:
  0.0 0.9 copy-start.2
  0.9 0.9 copy-start.3
  1.8 0.7 copy-start.4
  2.4 0.7 copy-start.5
  3.1 0.7 copy-start.6
  4.4 4.7 %collective-permute-start = (bf16[400,128]{1,0:T(8,128)(2,1)S(1)}, bf16[400,128]{1,0:T(8,128)(2,1)S(1)}, u32[]{:S(2)}, u32[]{:S(2)}) collective-permute-start(bf16[400,128]{1,0:T(8,128)(2,1)S(1)} %prepare_queries.1.refs_0_), channel_id=1, source_target_pairs={{0,4},{4,0},{8,12},{12,8},{16,20},{20,16},{24,28},{28,24},{32,36},... | collective-permute-start | bytes 307208 | tf_op jit(solution)/shard_map/ppermute | solution.py:338
  4.9 1.4 copy-start
  6.3 9.0 %copy-start.7 = (bf16[2048,384]{1,0:T(8,128)(2,1)S(1)}, bf16[2048,384]{1,0:T(8,128)(2,1)}, u32[]{:S(2)}) copy-start(bf16[2048,384]{1,0:T(8,128)(2,1)} %refs_1_.7) | copy-start | bytes 4718596
  6.3 9.0 %copy-start.8 = (f32[4]{0:T(128)S(1)}, f32[4]{0:T(128)}, u32[]{:S(2)}) copy-start(f32[4]{0:T(128)} %slopes_ref.9) | copy-start | bytes 52
  9.1 41.2 %collective-permute-start.7 = (bf16[2,400,128]{2,1,0:T(8,128)(2,1)S(1)}, bf16[2,400,128]{2,1,0:T(8,128)(2,1)S(1)}, u32[]{:S(2)}, u32[]{:S(2)}) collective-permute-start(bf16[2,400,128]{2,1,0:T(8,128)(2,1)S(1)} %pad_maximum_fusion), channel_id=1, source_target_pairs={{0,240},{4,244},{8,248},{12,252},{16,0},{20,4},{24,8},{28,12},{32,... | collective-permute-start | bytes 614408 | tf_op jit(solution)/shard_map/ppermute | solution.py:334
  9.8 48.3 %collective-permute-start.5 = (bf16[2,400,128]{2,1,0:T(8,128)(2,1)S(1)}, bf16[2,400,128]{2,1,0:T(8,128)(2,1)S(1)}, u32[]{:S(2)}, u32[]{:S(2)}) collective-permute-start(bf16[2,400,128]{2,1,0:T(8,128)(2,1)S(1)} %pad_maximum_fusion), channel_id=1, source_target_pairs={{0,16},{4,20},{8,24},{12,28},{16,32},{20,36},{24,40},{28,44},{32,4... | collective-permute-start | bytes 614408 | tf_op jit(solution)/shard_map/ppermute | solution.py:334
  12.1 48.8 %collective-permute-start.3 = (bf16[2,400,128]{2,1,0:T(8,128)(2,1)S(1)}, bf16[2,400,128]{2,1,0:T(8,128)(2,1)S(1)}, u32[]{:S(2)}, u32[]{:S(2)}) collective-permute-start(bf16[2,400,128]{2,1,0:T(8,128)(2,1)S(1)} %pad_maximum_fusion), channel_id=1, source_target_pairs={{0,248},{4,252},{8,0},{12,4},{16,8},{20,12},{24,16},{28,20},{32,24... | collective-permute-start | bytes 614408 | tf_op jit(solution)/shard_map/ppermute | solution.py:334
  13.1 111.7 %collective-permute-start.1 = (bf16[2,400,128]{2,1,0:T(8,128)(2,1)S(1)}, bf16[2,400,128]{2,1,0:T(8,128)(2,1)S(1)}, u32[]{:S(2)}, u32[]{:S(2)}) collective-permute-start(bf16[2,400,128]{2,1,0:T(8,128)(2,1)S(1)} %pad_maximum_fusion), channel_id=1, source_target_pairs={{0,8},{4,12},{8,16},{12,20},{16,24},{20,28},{24,32},{28,36},{32,40... | collective-permute-start | bytes 614408 | tf_op jit(solution)/shard_map/ppermute | solution.py:334
  53.2 106.6 %collective-permute-start.8 = (bf16[2,400,128]{2,1,0:T(8,128)(2,1)S(1)}, bf16[2,400,128]{2,1,0:T(8,128)(2,1)S(1)}, u32[]{:S(2)}, u32[]{:S(2)}) collective-permute-start(bf16[2,400,128]{2,1,0:T(8,128)(2,1)S(1)} %attend_near.9), channel_id=1, source_target_pairs={{0,16},{4,20},{8,24},{12,28},{16,32},{20,36},{24,40},{28,44},{32,4... | collective-permute-start | bytes 614408 | tf_op jit(solution)/shard_map/ppermute | solution.py:334
  60.8 99.0 %collective-permute-start.6 = (bf16[2,400,128]{2,1,0:T(8,128)(2,1)S(1)}, bf16[2,400,128]{2,1,0:T(8,128)(2,1)S(1)}, u32[]{:S(2)}, u32[]{:S(2)}) collective-permute-start(bf16[2,400,128]{2,1,0:T(8,128)(2,1)S(1)} %attend_near.8), channel_id=1, source_target_pairs={{0,240},{4,244},{8,248},{12,252},{16,0},{20,4},{24,8},{28,12},{32,... | collective-permute-start | bytes 614408 | tf_op jit(solution)/shard_map/ppermute | solution.py:334
  95.8 74.6 %copy-start.1 = (bf16[384,1536]{1,0:T(8,128)(2,1)S(1)}, bf16[384,1536]{1,0:T(8,128)(2,1)}, u32[]{:S(2)}) copy-start(bf16[384,1536]{1,0:T(8,128)(2,1)} %refs_5_.1) | copy-start | bytes 3538948
  95.8 64.0 %collective-permute-start.4 = (bf16[2,400,128]{2,1,0:T(8,128)(2,1)S(1)}, bf16[2,400,128]{2,1,0:T(8,128)(2,1)S(1)}, u32[]{:S(2)}, u32[]{:S(2)}) collective-permute-start(bf16[2,400,128]{2,1,0:T(8,128)(2,1)S(1)} %attend_near.7), channel_id=1, source_target_pairs={{0,8},{4,12},{8,16},{12,20},{16,24},{20,28},{24,32},{28,36},{32,40... | collective-permute-start | bytes 614408 | tf_op jit(solution)/shard_map/ppermute | solution.py:334
  159.7 5.8 %collective-permute-start.2 = (bf16[2,400,128]{2,1,0:T(8,128)(2,1)S(1)}, bf16[2,400,128]{2,1,0:T(8,128)(2,1)S(1)}, u32[]{:S(2)}, u32[]{:S(2)}) collective-permute-start(bf16[2,400,128]{2,1,0:T(8,128)(2,1)S(1)} %attend_near.6), channel_id=1, source_target_pairs={{0,248},{4,252},{8,0},{12,4},{16,8},{20,12},{24,16},{28,20},{32,24... | collective-permute-start | bytes 614408 | tf_op jit(solution)/shard_map/ppermute | solution.py:334
  165.7 4.7 %collective-permute-start.9 = (bf16[400,128]{1,0:T(8,128)(2,1)S(1)}, bf16[400,128]{1,0:T(8,128)(2,1)S(1)}, u32[]{:S(2)}, u32[]{:S(2)}) collective-permute-start(bf16[400,128]{1,0:T(8,128)(2,1)S(1)} %merge_other.1), channel_id=1, source_target_pairs={{0,4},{4,0},{8,12},{12,8},{16,20},{20,16},{24,28},{28,24},{32,36},... | collective-permute-start | bytes 307208 | tf_op jit(solution)/shard_map/ppermute | solution.py:338
  171.0 1.5 collective-permute-start.10
  172.5 6.4 %collective-permute-start.11 = (bf16[128,384]{1,0:T(8,128)(2,1)S(1)}, bf16[128,384]{1,0:T(8,128)(2,1)S(1)}, u32[]{:S(2)}, u32[]{:S(2)}) collective-permute-start(bf16[128,384]{1,0:T(8,128)(2,1)S(1)} %fusion.1), channel_id=1, source_target_pairs={{0,2},{1,3},{2,0},{3,1},{4,6},{5,7},{6,4},{7,5},{8,10},{9,11},{10,... | collective-permute-start | bytes 294920 | tf_op jit(solution)/shard_map/ppermute | solution.py:338

commit v4 on v3

--- a/solution.py
+++ b/solution.py
@@ -19,7 +19,7 @@
 SUM_LO, SUM_HI = 2.0**-60, 2.0**100
 TILE = 512
 ORDER = (2, 3, 0, 1)
-QUERY_VMEM = 4 * 2**20
+QUERY_VMEM = 60 * 2**20
 EXTRA = 16
 
 SMEM = pl.BlockSpec(memory_space=pltpu.SMEM)

time: 181 us -> 184 us (1.017)
  the two profiles are of different devices: /device:TPU:168 before, /device:TPU:14 now
where the time goes in v4:
time: 184 us; the launch traced here: 185 us
  Pallas kernels  113 us (61%)
  starting transfers between devices  48.2 us (26%)
  waiting for transfers between devices  20.7 us (11%)
    pallas_call x5, Pallas kernels, attend_near(): pl.pallas_call(functools.partial(near_kernel, shifts, seq_count), in_spec...  110 us
    ppermute x8, starting transfers between devices, rotated(): lax.ppermute(value, 'seq', [(i, (i + steps) % count) for i in range(count)])  47.4 us
    ppermute x4, waiting for transfers between devices, swapped(): lax.ppermute(value, axis, [(i, i ^ bit) for i in range(lax.axis_size(axis...  14.9 us
    ppermute x8, waiting for transfers between devices, rotated(): lax.ppermute(value, 'seq', [(i, (i + steps) % count) for i in range(count)])  5.73 us
  transfers between devices with their start and end apart: 12, of which 5 were waited for; matrix products, arithmetic and copies ran while one was open for 0% of the time, Pallas kernels for 60%

profile of v4, /device:TPU:14, one launch (start us, length us, event | category | flops | bytes accessed | tf_op | source)
XLA Modules:
  0.0 184.6 jit_solution(17614613641794791765)
XLA Ops:
  0.0 2.0 %prepare_queries.1.refs_0_ = bf16[400,128]{1,0:T(8,128)(2,1)} custom-call(s32[1]{0:T(128)} %bitcast.2.base_ref, s32[1,128]{1,0:T(1,128)} %bitcast.16, s32[1,128]{1,0:T(1,128)} %bitcast.17, s32[1,128]{1,0:T(1,128)} %bitcast.18, bf16[128,384]{1,0:T(8,128)(2,1)} %refs_3_.1, bf16[128,384]{1,0:T(8,128)(2,1)} %refs_4_.1), custom_call_target="tpu_custom_call" | custom-call | tf_op jit(solution)/shard_map/prepare_queries/pallas_call | solution.py:263
  2.0 0.5 collective-permute-start
  2.5 1.4 copy-done
  3.9 0.5 prepare_bins.1.refs_3_.refs_2_
  4.4 2.5 %collective-permute-done.refs_1_ = bf16[400,128]{1,0:T(8,128)(2,1)S(1)} collective-permute-done((bf16[400,128]{1,0:T(8,128)(2,1)}, bf16[400,128]{1,0:T(8,128)(2,1)S(1)}, u32[]{:S(2)}, u32[]{:S(2)}) %collective-permute-start) | collective-permute-done | bytes 102432 | tf_op jit(solution)/shard_map/ppermute | solution.py:338
  7.0 6.6 %collective-permute-start.7 = (bf16[2,400,128]{2,1,0:T(8,128)(2,1)S(1)}, bf16[2,400,128]{2,1,0:T(8,128)(2,1)S(1)}, u32[]{:S(2)}, u32[]{:S(2)}) collective-permute-start(bf16[2,400,128]{2,1,0:T(8,128)(2,1)S(1)} %pad_maximum_fusion), channel_id=1, source_target_pairs={{0,240},{4,244},{8,248},{12,252},{16,0},{20,4},{24,8},{28,12},{32,... | collective-permute-start | bytes 614408 | tf_op jit(solution)/shard_map/ppermute | solution.py:334
  13.6 0.0 collective-permute-start.5
  13.6 4.6 %collective-permute-start.3 = (bf16[2,400,128]{2,1,0:T(8,128)(2,1)S(1)}, bf16[2,400,128]{2,1,0:T(8,128)(2,1)S(1)}, u32[]{:S(2)}, u32[]{:S(2)}) collective-permute-start(bf16[2,400,128]{2,1,0:T(8,128)(2,1)S(1)} %pad_maximum_fusion), channel_id=1, source_target_pairs={{0,248},{4,252},{8,0},{12,4},{16,8},{20,12},{24,16},{28,20},{32,24... | collective-permute-start | bytes 614408 | tf_op jit(solution)/shard_map/ppermute | solution.py:334
  18.2 0.0 collective-permute-start.1
  18.2 35.0 %attend_near.5.refs_0_ = bf16[2,400,128]{2,1,0:T(8,128)(2,1)S(1)} custom-call(f32[4]{0:T(128)S(1)} %copy-done.4, s32[1]{0:T(128)} %bitcast.1.position_ref, bf16[400,128]{1,0:T(8,128)(2,1)S(1)} %copy-done.2, bf16[400,128]{1,0:T(8,128)(2,1)S(1)} %collective-permute-done.refs_1_, bf16[2048,384]{1,0:T(8,128)(2,1)S(1)} %copy-done.3, ...), custom_call_target="tpu_custom_call" | custom-call | flops 1073741824 | bytes 4194304 | tf_op jit(solution)/shard_map/attend_near/pallas_call | solution.py:291
  53.3 2.8 %attend_near.9 = bf16[2,400,128]{2,1,0:T(8,128)(2,1)S(1)} custom-call(f32[4]{0:T(128)S(1)} %copy-done.4, s32[1]{0:T(128)} %bitcast.1.position_ref, bf16[2,400,128]{2,1,0:T(8,128)(2,1)S(1)} %collective-permute-done.7.refs_0_, bf16[2048,384]{1,0:T(8,128)(2,1)S(1)} %copy-done.3, bf16[4,112,2048]{2,1,0:T(8,128)(2,1)S(1)} %prepare_bins.1.refs_3_.refs_2_), custom_call_target="tpu_custom_call" | custom-call | flops 1073741824 | bytes 4194304 | tf_op jit(solution)/shard_map/attend_near/pallas_call | solution.py:291
  56.1 0.3 collective-permute-start.8
  56.3 2.7 %attend_near.8 = bf16[2,400,128]{2,1,0:T(8,128)(2,1)S(1)} custom-call(f32[4]{0:T(128)S(1)} %copy-done.4, s32[1]{0:T(128)} %bitcast.1.position_ref, bf16[2,400,128]{2,1,0:T(8,128)(2,1)S(1)} %collective-permute-done.5.refs_0_, bf16[2048,384]{1,0:T(8,128)(2,1)S(1)} %copy-done.3, bf16[4,112,2048]{2,1,0:T(8,128)(2,1)S(1)} %prepare_bins.1.refs_3_.refs_2_), custom_call_target="tpu_custom_call" | custom-call | flops 1073741824 | bytes 4194304 | tf_op jit(solution)/shard_map/attend_near/pallas_call | solution.py:291
  59.1 5.1 %collective-permute-start.6 = (bf16[2,400,128]{2,1,0:T(8,128)(2,1)S(1)}, bf16[2,400,128]{2,1,0:T(8,128)(2,1)S(1)}, u32[]{:S(2)}, u32[]{:S(2)}) collective-permute-start(bf16[2,400,128]{2,1,0:T(8,128)(2,1)S(1)} %attend_near.8), channel_id=1, source_target_pairs={{0,240},{4,244},{8,248},{12,252},{16,0},{20,4},{24,8},{28,12},{32,... | collective-permute-start | bytes 614408 | tf_op jit(solution)/shard_map/ppermute | solution.py:334
  64.2 0.0 collective-permute-done.3.refs_0_
  64.2 34.9 %attend_near.7 = bf16[2,400,128]{2,1,0:T(8,128)(2,1)S(1)} custom-call(f32[4]{0:T(128)S(1)} %copy-done.4, s32[1]{0:T(128)} %bitcast.1.position_ref, bf16[2,400,128]{2,1,0:T(8,128)(2,1)S(1)} %collective-permute-done.3.refs_0_, bf16[2048,384]{1,0:T(8,128)(2,1)S(1)} %copy-done.3, bf16[4,112,2048]{2,1,0:T(8,128)(2,1)S(1)} %prepare_bins.1.refs_3_.refs_2_), custom_call_target="tpu_custom_call" | custom-call | flops 1073741824 | bytes 4194304 | tf_op jit(solution)/shard_map/attend_near/pallas_call | solution.py:291
  99.1 0.0 copy-start.1
  99.1 30.7 %collective-permute-start.4 = (bf16[2,400,128]{2,1,0:T(8,128)(2,1)S(1)}, bf16[2,400,128]{2,1,0:T(8,128)(2,1)S(1)}, u32[]{:S(2)}, u32[]{:S(2)}) collective-permute-start(bf16[2,400,128]{2,1,0:T(8,128)(2,1)S(1)} %attend_near.7), channel_id=1, source_target_pairs={{0,8},{4,12},{8,16},{12,20},{16,24},{20,28},{24,32},{28,36},{32,40... | collective-permute-start | bytes 614408 | tf_op jit(solution)/shard_map/ppermute | solution.py:334
  129.8 34.9 %attend_near.6 = bf16[2,400,128]{2,1,0:T(8,128)(2,1)S(1)} custom-call(f32[4]{0:T(128)S(1)} %copy-done.4, s32[1]{0:T(128)} %bitcast.1.position_ref, bf16[2,400,128]{2,1,0:T(8,128)(2,1)S(1)} %collective-permute-done.1.refs_0_, bf16[2048,384]{1,0:T(8,128)(2,1)S(1)} %copy-done.3, bf16[4,112,2048]{2,1,0:T(8,128)(2,1)S(1)} %prepare_bins.1.refs_3_.refs_2_), custom_call_target="tpu_custom_call" | custom-call | flops 1073741824 | bytes 4194304 | tf_op jit(solution)/shard_map/attend_near/pallas_call | solution.py:291
  164.7 0.1 collective-permute-start.2
  164.8 0.0 collective-permute-done.8.refs_4_
  164.8 0.0 collective-permute-done.6.refs_3_
  164.8 5.7 %collective-permute-done.2.refs_1_ = bf16[2,400,128]{2,1,0:T(8,128)(2,1)S(1)} collective-permute-done((bf16[2,400,128]{2,1,0:T(8,128)(2,1)S(1)}, bf16[2,400,128]{2,1,0:T(8,128)(2,1)S(1)}, u32[]{:S(2)}, u32[]{:S(2)}) %collective-permute-start.2) | collective-permute-done | bytes 204832 | tf_op jit(solution)/shard_map/ppermute | solution.py:334
  170.5 0.1 merge_other.1
  170.6 0.1 collective-permute-start.9
  170.7 4.6 %collective-permute-done.9.theirs_ref = bf16[400,128]{1,0:T(8,128)(2,1)S(1)} collective-permute-done((bf16[400,128]{1,0:T(8,128)(2,1)S(1)}, bf16[400,128]{1,0:T(8,128)(2,1)S(1)}, u32[]{:S(2)}, u32[]{:S(2)}) %collective-permute-start.9) | collective-permute-done | bytes 102432 | tf_op jit(solution)/shard_map/ppermute | solution.py:338
  175.4 0.6 merge.1
  176.0 0.1 collective-permute-start.10
  176.1 1.4 collective-permute-done.10
  177.5 0.1 collective-permute-start.11
  177.6 6.3 %collective-permute-done.11 = bf16[128,384]{1,0:T(8,128)(2,1)S(1)} collective-permute-done((bf16[128,384]{1,0:T(8,128)(2,1)S(1)}, bf16[128,384]{1,0:T(8,128)(2,1)S(1)}, u32[]{:S(2)}, u32[]{:S(2)}) %collective-permute-start.11) | collective-permute-done | bytes 98336 | tf_op jit(solution)/shard_map/ppermute | solution.py:338
  183.9 0.7 fusion
  (14 shorter events, 0.1 us)
Async XLA Ops:
  2.0 5.0 %collective-permute-start = (bf16[400,128]{1,0:T(8,128)(2,1)}, bf16[400,128]{1,0:T(8,128)(2,1)S(1)}, u32[]{:S(2)}, u32[]{:S(2)}) collective-permute-start(bf16[400,128]{1,0:T(8,128)(2,1)} %prepare_queries.1.refs_0_), channel_id=1, source_target_pairs={{0,4},{4,0},{8,12},{12,8},{16,20},{20,16},{24,28},{28,24},{32,36},... | collective-permute-start | bytes 307208 | tf_op jit(solution)/shard_map/ppermute | solution.py:338
  2.5 1.4 copy-start
  3.9 3.0 %copy-start.2 = (bf16[400,128]{1,0:T(8,128)(2,1)S(1)}, bf16[400,128]{1,0:T(8,128)(2,1)}, u32[]{:S(2)}) copy-start(bf16[400,128]{1,0:T(8,128)(2,1)} %prepare_queries.1.refs_0_) | copy-start | bytes 307204
  3.9 14.3 %copy-start.3 = (bf16[2048,384]{1,0:T(8,128)(2,1)S(1)}, bf16[2048,384]{1,0:T(8,128)(2,1)}, u32[]{:S(2)}) copy-start(bf16[2048,384]{1,0:T(8,128)(2,1)} %refs_1_.7) | copy-start | bytes 4718596
  3.9 14.3 %copy-start.4 = (f32[4]{0:T(128)S(1)}, f32[4]{0:T(128)}, u32[]{:S(2)}) copy-start(f32[4]{0:T(128)} %slopes_ref.9) | copy-start | bytes 52
  7.0 46.3 %collective-permute-start.7 = (bf16[2,400,128]{2,1,0:T(8,128)(2,1)S(1)}, bf16[2,400,128]{2,1,0:T(8,128)(2,1)S(1)}, u32[]{:S(2)}, u32[]{:S(2)}) collective-permute-start(bf16[2,400,128]{2,1,0:T(8,128)(2,1)S(1)} %pad_maximum_fusion), channel_id=1, source_target_pairs={{0,240},{4,244},{8,248},{12,252},{16,0},{20,4},{24,8},{28,12},{32,... | collective-permute-start | bytes 614408 | tf_op jit(solution)/shard_map/ppermute | solution.py:334
  13.6 42.7 %collective-permute-start.5 = (bf16[2,400,128]{2,1,0:T(8,128)(2,1)S(1)}, bf16[2,400,128]{2,1,0:T(8,128)(2,1)S(1)}, u32[]{:S(2)}, u32[]{:S(2)}) collective-permute-start(bf16[2,400,128]{2,1,0:T(8,128)(2,1)S(1)} %pad_maximum_fusion), channel_id=1, source_target_pairs={{0,16},{4,20},{8,24},{12,28},{16,32},{20,36},{24,40},{28,44},{32,4... | collective-permute-start | bytes 614408 | tf_op jit(solution)/shard_map/ppermute | solution.py:334
  13.6 50.6 %collective-permute-start.3 = (bf16[2,400,128]{2,1,0:T(8,128)(2,1)S(1)}, bf16[2,400,128]{2,1,0:T(8,128)(2,1)S(1)}, u32[]{:S(2)}, u32[]{:S(2)}) collective-permute-start(bf16[2,400,128]{2,1,0:T(8,128)(2,1)S(1)} %pad_maximum_fusion), channel_id=1, source_target_pairs={{0,248},{4,252},{8,0},{12,4},{16,8},{20,12},{24,16},{28,20},{32,24... | collective-permute-start | bytes 614408 | tf_op jit(solution)/shard_map/ppermute | solution.py:334
  18.2 111.6 %collective-permute-start.1 = (bf16[2,400,128]{2,1,0:T(8,128)(2,1)S(1)}, bf16[2,400,128]{2,1,0:T(8,128)(2,1)S(1)}, u32[]{:S(2)}, u32[]{:S(2)}) collective-permute-start(bf16[2,400,128]{2,1,0:T(8,128)(2,1)S(1)} %pad_maximum_fusion), channel_id=1, source_target_pairs={{0,8},{4,12},{8,16},{12,20},{16,24},{20,28},{24,32},{28,36},{32,40... | collective-permute-start | bytes 614408 | tf_op jit(solution)/shard_map/ppermute | solution.py:334
  56.1 108.7 %collective-permute-start.8 = (bf16[2,400,128]{2,1,0:T(8,128)(2,1)S(1)}, bf16[2,400,128]{2,1,0:T(8,128)(2,1)S(1)}, u32[]{:S(2)}, u32[]{:S(2)}) collective-permute-start(bf16[2,400,128]{2,1,0:T(8,128)(2,1)S(1)} %attend_near.9), channel_id=1, source_target_pairs={{0,16},{4,20},{8,24},{12,28},{16,32},{20,36},{24,40},{28,44},{32,4... | collective-permute-start | bytes 614408 | tf_op jit(solution)/shard_map/ppermute | solution.py:334
  59.1 105.7 %collective-permute-start.6 = (bf16[2,400,128]{2,1,0:T(8,128)(2,1)S(1)}, bf16[2,400,128]{2,1,0:T(8,128)(2,1)S(1)}, u32[]{:S(2)}, u32[]{:S(2)}) collective-permute-start(bf16[2,400,128]{2,1,0:T(8,128)(2,1)S(1)} %attend_near.8), channel_id=1, source_target_pairs={{0,240},{4,244},{8,248},{12,252},{16,0},{20,4},{24,8},{28,12},{32,... | collective-permute-start | bytes 614408 | tf_op jit(solution)/shard_map/ppermute | solution.py:334
  99.1 76.3 %copy-start.1 = (bf16[384,1536]{1,0:T(8,128)(2,1)S(1)}, bf16[384,1536]{1,0:T(8,128)(2,1)}, u32[]{:S(2)}) copy-start(bf16[384,1536]{1,0:T(8,128)(2,1)} %refs_5_.1) | copy-start | bytes 3538948
  99.1 65.7 %collective-permute-start.4 = (bf16[2,400,128]{2,1,0:T(8,128)(2,1)S(1)}, bf16[2,400,128]{2,1,0:T(8,128)(2,1)S(1)}, u32[]{:S(2)}, u32[]{:S(2)}) collective-permute-start(bf16[2,400,128]{2,1,0:T(8,128)(2,1)S(1)} %attend_near.7), channel_id=1, source_target_pairs={{0,8},{4,12},{8,16},{12,20},{16,24},{20,28},{24,32},{28,36},{32,40... | collective-permute-start | bytes 614408 | tf_op jit(solution)/shard_map/ppermute | solution.py:334
  164.7 5.8 %collective-permute-start.2 = (bf16[2,400,128]{2,1,0:T(8,128)(2,1)S(1)}, bf16[2,400,128]{2,1,0:T(8,128)(2,1)S(1)}, u32[]{:S(2)}, u32[]{:S(2)}) collective-permute-start(bf16[2,400,128]{2,1,0:T(8,128)(2,1)S(1)} %attend_near.6), channel_id=1, source_target_pairs={{0,248},{4,252},{8,0},{12,4},{16,8},{20,12},{24,16},{28,20},{32,24... | collective-permute-start | bytes 614408 | tf_op jit(solution)/shard_map/ppermute | solution.py:334
  170.6 4.7 %collective-permute-start.9 = (bf16[400,128]{1,0:T(8,128)(2,1)S(1)}, bf16[400,128]{1,0:T(8,128)(2,1)S(1)}, u32[]{:S(2)}, u32[]{:S(2)}) collective-permute-start(bf16[400,128]{1,0:T(8,128)(2,1)S(1)} %merge_other.1), channel_id=1, source_target_pairs={{0,4},{4,0},{8,12},{12,8},{16,20},{20,16},{24,28},{28,24},{32,36},... | collective-permute-start | bytes 307208 | tf_op jit(solution)/shard_map/ppermute | solution.py:338
  176.0 1.5 collective-permute-start.10
  177.5 6.4 %collective-permute-start.11 = (bf16[128,384]{1,0:T(8,128)(2,1)S(1)}, bf16[128,384]{1,0:T(8,128)(2,1)S(1)}, u32[]{:S(2)}, u32[]{:S(2)}) collective-permute-start(bf16[128,384]{1,0:T(8,128)(2,1)S(1)} %fusion.1), channel_id=1, source_target_pairs={{0,2},{1,3},{2,0},{3,1},{4,6},{5,7},{6,4},{7,5},{8,10},{9,11},{10,... | collective-permute-start | bytes 294920 | tf_op jit(solution)/shard_map/ppermute | solution.py:338

commit v5 on v4

--- a/solution.py
+++ b/solution.py
@@ -18,7 +18,6 @@
 EMPTY = -16384.0
 SUM_LO, SUM_HI = 2.0**-60, 2.0**100
 TILE = 512
-ORDER = (2, 3, 0, 1)
 QUERY_VMEM = 60 * 2**20
 EXTRA = 16
 
@@ -191,15 +190,14 @@
 
 def near_kernel(shifts, seq_count, slopes_ref, position_ref, *refs):
     query_refs, (keys_ref, values_ref, out_ref, acc_ref) = refs[:-4], refs[-4:]
-    if len(query_refs) == 1:
+    if len(query_refs[0].shape) == 3:
         query_refs = [query_refs[0].at[i] for i in range(len(shifts))]
     position = position_ref[0]
     odd = position & 1
     blocks, strides, oks = [], [], []
-    for shift, same in shifts:
-        block = (2 * shift,) if same else (2 * shift - 1, 2 * shift + 1)
-        stride = jnp.int32(2 * shift) if same else 2 * shift + 2 * odd - 1
-        blocks.append(block)
+    for even_stride, odd_stride in shifts:
+        stride = even_stride + (odd_stride - even_stride) * odd
+        blocks.append(tuple(sorted({even_stride, odd_stride})))
         strides.append(stride)
         oks.append((position - stride >= 0) & (position - stride < seq_count))
     attend_rows(
@@ -329,9 +327,10 @@
     )(place[None], theirs, *parts, w_out)
 
 
-def rotated(value, steps):
+def rotated(value, steps, mirrored=False):
     count = lax.axis_size("seq")
-    return lax.ppermute(value, "seq", [(i, (i + steps) % count) for i in range(count)])
+    moves = [-steps if mirrored and i % 2 else steps for i in range(count)]
+    return lax.ppermute(value, "seq", [(i, (i + move) % count) for i, move in enumerate(moves)])
 
 
 def swapped(value, axis, bit):
@@ -350,19 +349,15 @@
     values = prepare_bins(bin_values, groups)
     other, values = lax.optimization_barrier((other, values))
     both = jnp.stack([mine, other])
-    shifts = [2, -2, 1, -1]
-    arrived = [rotated(both, 2 * shift) for shift in shifts]
-    part = attend_near(((0, True), (0, False)), seq_count, slopes, position, [mine, other], bin_keys, values)
-    parts = [part]
-    for k in ORDER:
-        shift = shifts[k]
-        query = arrived[k]
-        if k == ORDER[0]:
-            query, _ = lax.optimization_barrier((query, part))
-        share = attend_near(((shift, True), (shift, False)), seq_count, slopes, position, [query], bin_keys, values)
-        parts.append(rotated(share, -2 * shift))
+    outward = [rotated(both, 4, True), rotated(mine, -4, True), rotated(both, 2), rotated(both, -2)]
+    reach = [((4, -4), (3, -3)), ((-4, 4),), ((2, 2), (1, 3)), ((-2, -2), (-3, -1))]
+    back = [(-4, True), (4, True), (-2, False), (2, False)]
+    home = attend_near(((0, 0), (-1, 1)), seq_count, slopes, position, [mine, other], bin_keys, values)
+    shares = [attend_near(blocks, seq_count, slopes, position, [query], bin_keys, values) for query, blocks in zip(outward, reach)]
+    far, farther, up, down = [rotated(share, *steps) for share, steps in zip(shares, back)]
+    parts = [home, up, down, far]
     theirs = swapped(merge_other(parts, groups), "seq", 1)
-    keep, send = merge(place, theirs, parts, w_out, groups)
+    keep, send = merge(place, theirs, parts + [farther], w_out, groups)
     got = swapped(send, "head", 1)
     rest = (keep[1] + got[1].astype(jnp.float32)).astype(jnp.bfloat16)
     last = swapped(rest, "head", 2)

time: 184 us -> 175 us (0.951)
  the two profiles are of different devices: /device:TPU:14 before, /device:TPU:188 now
where the time goes in v5:
time: 175 us; the launch traced here: 174 us
  Pallas kernels  80.9 us (46%)
  starting transfers between devices  72 us (41%)
  waiting for transfers between devices  19 us (11%)
    pallas_call x5, Pallas kernels, attend_near(): pl.pallas_call(functools.partial(near_kernel, shifts, seq_count), in_spec...  77.8 us
    ppermute x4, starting transfers between devices, swapped(): lax.ppermute(value, axis, [(i, i ^ bit) for i in range(lax.axis_size(axis...  55.9 us
    ppermute x8, starting transfers between devices, rotated(): lax.ppermute(value, 'seq', [(i, (i + move) % count) for i, move in enumer...  16.1 us
    ppermute x4, waiting for transfers between devices, swapped(): lax.ppermute(value, axis, [(i, i ^ bit) for i in range(lax.axis_size(axis...  14.5 us
    ppermute x8, waiting for transfers between devices, rotated(): lax.ppermute(value, 'seq', [(i, (i + move) % count) for i, move in enumer...  4.55 us
  transfers between devices with their start and end apart: 12, of which 5 were waited for; matrix products, arithmetic and copies ran while one was open for 0% of the time, Pallas kernels for 45%

profile of v5, /device:TPU:188, one launch (start us, length us, event | category | flops | bytes accessed | tf_op | source)
XLA Modules:
  0.0 174.3 jit_solution(6123613428901951531)
XLA Ops:
  0.0 2.0 %prepare_queries.1.refs_0_ = bf16[400,128]{1,0:T(8,128)(2,1)} custom-call(s32[1]{0:T(128)} %bitcast.2.base_ref, s32[1,128]{1,0:T(1,128)} %bitcast.16, s32[1,128]{1,0:T(1,128)} %bitcast.17, s32[1,128]{1,0:T(1,128)} %bitcast.18, bf16[128,384]{1,0:T(8,128)(2,1)} %refs_3_.1, bf16[128,384]{1,0:T(8,128)(2,1)} %refs_4_.1), custom_call_target="tpu_custom_call" | custom-call | tf_op jit(solution)/shard_map/prepare_queries/pallas_call | solution.py:261
  2.0 0.8 collective-permute-start
  2.8 1.4 copy-done
  4.2 0.5 prepare_bins.1.refs_3_.refs_2_
  4.7 2.2 %collective-permute-done.refs_1_ = bf16[400,128]{1,0:T(8,128)(2,1)S(1)} collective-permute-done((bf16[400,128]{1,0:T(8,128)(2,1)}, bf16[400,128]{1,0:T(8,128)(2,1)S(1)}, u32[]{:S(2)}, u32[]{:S(2)}) %collective-permute-start) | collective-permute-done | bytes 102432 | tf_op jit(solution)/shard_map/ppermute | solution.py:337
  7.0 0.6 collective-permute-start.5
  7.6 0.5 collective-permute-start.3
  8.2 1.5 collective-permute-start.1
  9.6 4.5 %collective-permute-start.8 = (bf16[400,128]{1,0:T(8,128)(2,1)S(1)}, bf16[400,128]{1,0:T(8,128)(2,1)S(1)}, u32[]{:S(2)}, u32[]{:S(2)}) collective-permute-start(bf16[400,128]{1,0:T(8,128)(2,1)S(1)} %copy-done.3), channel_id=1, source_target_pairs={{0,240},{4,20},{8,248},{12,28},{16,0},{20,36},{24,8},{28,44},{32,1... | collective-permute-start | bytes 307208 | tf_op jit(solution)/shard_map/ppermute | solution.py:333
  14.1 4.5 %collective-permute-done.5.refs_0_ = bf16[2,400,128]{2,1,0:T(8,128)(2,1)S(1)} collective-permute-done((bf16[2,400,128]{2,1,0:T(8,128)(2,1)S(1)}, bf16[2,400,128]{2,1,0:T(8,128)(2,1)S(1)}, u32[]{:S(2)}, u32[]{:S(2)}) %collective-permute-start.5) | collective-permute-done | bytes 204832 | tf_op jit(solution)/shard_map/ppermute | solution.py:333
  18.7 3.0 %attend_near.8 = bf16[2,400,128]{2,1,0:T(8,128)(2,1)S(1)} custom-call(f32[4]{0:T(128)S(1)} %copy-done.4, s32[1]{0:T(128)} %bitcast.1.position_ref, bf16[2,400,128]{2,1,0:T(8,128)(2,1)S(1)} %collective-permute-done.5.refs_0_, bf16[2048,384]{1,0:T(8,128)(2,1)S(1)} %copy-done.1, bf16[4,112,2048]{2,1,0:T(8,128)(2,1)S(1)} %prepare_bins.1.refs_3_.refs_2_), custom_call_target="tpu_custom_call" | custom-call | flops 1073741824 | bytes 4194304 | tf_op jit(solution)/shard_map/attend_near/pallas_call | solution.py:289
  21.7 2.4 %collective-permute-start.6 = (bf16[2,400,128]{2,1,0:T(8,128)(2,1)S(1)}, bf16[2,400,128]{2,1,0:T(8,128)(2,1)S(1)}, u32[]{:S(2)}, u32[]{:S(2)}) collective-permute-start(bf16[2,400,128]{2,1,0:T(8,128)(2,1)S(1)} %attend_near.8), channel_id=1, source_target_pairs={{0,240},{4,20},{8,248},{12,28},{16,0},{20,36},{24,8},{28,44},{32,1... | collective-permute-start | bytes 614408 | tf_op jit(solution)/shard_map/ppermute | solution.py:333
  24.1 0.0 collective-permute-done.3.refs_0_
  24.1 34.8 %attend_near.7 = bf16[2,400,128]{2,1,0:T(8,128)(2,1)S(1)} custom-call(f32[4]{0:T(128)S(1)} %copy-done.4, s32[1]{0:T(128)} %bitcast.1.position_ref, bf16[2,400,128]{2,1,0:T(8,128)(2,1)S(1)} %collective-permute-done.3.refs_0_, bf16[2048,384]{1,0:T(8,128)(2,1)S(1)} %copy-done.1, bf16[4,112,2048]{2,1,0:T(8,128)(2,1)S(1)} %prepare_bins.1.refs_3_.refs_2_), custom_call_target="tpu_custom_call" | custom-call | flops 1073741824 | bytes 4194304 | tf_op jit(solution)/shard_map/attend_near/pallas_call | solution.py:289
  58.9 2.3 %collective-permute-start.4 = (bf16[2,400,128]{2,1,0:T(8,128)(2,1)S(1)}, bf16[2,400,128]{2,1,0:T(8,128)(2,1)S(1)}, u32[]{:S(2)}, u32[]{:S(2)}) collective-permute-start(bf16[2,400,128]{2,1,0:T(8,128)(2,1)S(1)} %attend_near.7), channel_id=1, source_target_pairs={{0,8},{4,12},{8,16},{12,20},{16,24},{20,28},{24,32},{28,36},{32,40... | collective-permute-start | bytes 614408 | tf_op jit(solution)/shard_map/ppermute | solution.py:333
  61.2 0.0 collective-permute-done.1.refs_0_
  61.2 2.6 %attend_near.6 = bf16[2,400,128]{2,1,0:T(8,128)(2,1)S(1)} custom-call(f32[4]{0:T(128)S(1)} %copy-done.4, s32[1]{0:T(128)} %bitcast.1.position_ref, bf16[2,400,128]{2,1,0:T(8,128)(2,1)S(1)} %collective-permute-done.1.refs_0_, bf16[2048,384]{1,0:T(8,128)(2,1)S(1)} %copy-done.1, bf16[4,112,2048]{2,1,0:T(8,128)(2,1)S(1)} %prepare_bins.1.refs_3_.refs_2_), custom_call_target="tpu_custom_call" | custom-call | flops 1073741824 | bytes 4194304 | tf_op jit(solution)/shard_map/attend_near/pallas_call | solution.py:289
  63.8 1.5 collective-permute-start.2
  65.4 0.0 collective-permute-done.8.refs_0_
  65.4 2.4 %attend_near.9 = bf16[1,400,128]{2,1,0:T(8,128)(2,1)S(1)} custom-call(f32[4]{0:T(128)S(1)} %copy-done.4, s32[1]{0:T(128)} %bitcast.1.position_ref, bf16[400,128]{1,0:T(8,128)(2,1)S(1)} %collective-permute-done.8.refs_0_, bf16[2048,384]{1,0:T(8,128)(2,1)S(1)} %copy-done.1, bf16[4,112,2048]{2,1,0:T(8,128)(2,1)S(1)} %prepare_bins.1.refs_3_.refs_2_), custom_call_target="tpu_custom_call" | custom-call | flops 536870912 | bytes 4194304 | tf_op jit(solution)/shard_map/attend_near/pallas_call | solution.py:289
  67.8 0.0 copy-start.2
  67.8 2.8 %collective-permute-start.9 = (bf16[1,400,128]{2,1,0:T(8,128)(2,1)S(1)}, bf16[1,400,128]{2,1,0:T(8,128)(2,1)S(1)}, u32[]{:S(2)}, u32[]{:S(2)}) collective-permute-start(bf16[1,400,128]{2,1,0:T(8,128)(2,1)S(1)} %attend_near.9), channel_id=1, source_target_pairs={{0,16},{4,244},{8,24},{12,252},{16,32},{20,4},{24,40},{28,12},{32,... | collective-permute-start | bytes 307208 | tf_op jit(solution)/shard_map/ppermute | solution.py:333
  70.5 35.0 %attend_near.5.refs_0_ = bf16[2,400,128]{2,1,0:T(8,128)(2,1)S(1)} custom-call(f32[4]{0:T(128)S(1)} %copy-done.4, s32[1]{0:T(128)} %bitcast.1.position_ref, bf16[400,128]{1,0:T(8,128)(2,1)S(1)} %copy-done.3, bf16[400,128]{1,0:T(8,128)(2,1)S(1)} %collective-permute-done.refs_1_, bf16[2048,384]{1,0:T(8,128)(2,1)S(1)} %copy-done.1, ...), custom_call_target="tpu_custom_call" | custom-call | flops 1073741824 | bytes 4194304 | tf_op jit(solution)/shard_map/attend_near/pallas_call | solution.py:289
  105.5 0.1 merge_other.1
  105.6 0.1 collective-permute-start.7
  105.8 4.6 %collective-permute-done.7.theirs_ref = bf16[400,128]{1,0:T(8,128)(2,1)S(1)} collective-permute-done((bf16[400,128]{1,0:T(8,128)(2,1)S(1)}, bf16[400,128]{1,0:T(8,128)(2,1)S(1)}, u32[]{:S(2)}, u32[]{:S(2)}) %collective-permute-start.7) | collective-permute-done | bytes 102432 | tf_op jit(solution)/shard_map/ppermute | solution.py:337
  110.4 0.6 merge.1
  111.0 54.9 %collective-permute-start.10 = (bf16[2,128,384]{2,1,0:T(8,128)(2,1)S(1)}, bf16[2,128,384]{2,1,0:T(8,128)(2,1)S(1)}, u32[]{:S(2)}, u32[]{:S(2)}) collective-permute-start(bf16[2,128,384]{2,1,0:T(8,128)(2,1)S(1)} %get-tuple-element.12), channel_id=1, source_target_pairs={{0,1},{1,0},{2,3},{3,2},{4,5},{5,4},{6,7},{7,6},{8,9},{9,8},{10,11... | collective-permute-start | bytes 589832 | tf_op jit(solution)/shard_map/ppermute | solution.py:337
  165.9 1.1 collective-permute-done.10
  167.0 0.1 collective-permute-start.11
  167.1 6.6 %collective-permute-done.11 = bf16[128,384]{1,0:T(8,128)(2,1)S(1)} collective-permute-done((bf16[128,384]{1,0:T(8,128)(2,1)S(1)}, bf16[128,384]{1,0:T(8,128)(2,1)S(1)}, u32[]{:S(2)}, u32[]{:S(2)}) %collective-permute-start.11) | collective-permute-done | bytes 98336 | tf_op jit(solution)/shard_map/ppermute | solution.py:337
  173.6 0.7 fusion
  (14 shorter events, 0.1 us)
Async XLA Ops:
  2.0 5.0 %collective-permute-start = (bf16[400,128]{1,0:T(8,128)(2,1)}, bf16[400,128]{1,0:T(8,128)(2,1)S(1)}, u32[]{:S(2)}, u32[]{:S(2)}) collective-permute-start(bf16[400,128]{1,0:T(8,128)(2,1)} %prepare_queries.1.refs_0_), channel_id=1, source_target_pairs={{0,4},{4,0},{8,12},{12,8},{16,20},{20,16},{24,28},{28,24},{32,36},... | collective-permute-start | bytes 307208 | tf_op jit(solution)/shard_map/ppermute | solution.py:337
  2.8 1.4 copy-start
  4.2 2.7 %copy-start.3 = (bf16[400,128]{1,0:T(8,128)(2,1)S(1)}, bf16[400,128]{1,0:T(8,128)(2,1)}, u32[]{:S(2)}) copy-start(bf16[400,128]{1,0:T(8,128)(2,1)} %prepare_queries.1.refs_0_) | copy-start | bytes 307204
  4.2 14.4 %copy-start.1 = (bf16[2048,384]{1,0:T(8,128)(2,1)S(1)}, bf16[2048,384]{1,0:T(8,128)(2,1)}, u32[]{:S(2)}) copy-start(bf16[2048,384]{1,0:T(8,128)(2,1)} %refs_1_.7) | copy-start | bytes 4718596
  4.2 14.4 %copy-start.4 = (f32[4]{0:T(128)S(1)}, f32[4]{0:T(128)}, u32[]{:S(2)}) copy-start(f32[4]{0:T(128)} %slopes_ref.9) | copy-start | bytes 52
  7.0 11.7 %collective-permute-start.5 = (bf16[2,400,128]{2,1,0:T(8,128)(2,1)S(1)}, bf16[2,400,128]{2,1,0:T(8,128)(2,1)S(1)}, u32[]{:S(2)}, u32[]{:S(2)}) collective-permute-start(bf16[2,400,128]{2,1,0:T(8,128)(2,1)S(1)} %pad_maximum_fusion), channel_id=1, source_target_pairs={{0,16},{4,244},{8,24},{12,252},{16,32},{20,4},{24,40},{28,12},{32,... | collective-permute-start | bytes 614408 | tf_op jit(solution)/shard_map/ppermute | solution.py:333
  7.6 16.5 %collective-permute-start.3 = (bf16[2,400,128]{2,1,0:T(8,128)(2,1)S(1)}, bf16[2,400,128]{2,1,0:T(8,128)(2,1)S(1)}, u32[]{:S(2)}, u32[]{:S(2)}) collective-permute-start(bf16[2,400,128]{2,1,0:T(8,128)(2,1)S(1)} %pad_maximum_fusion), channel_id=1, source_target_pairs={{0,248},{4,252},{8,0},{12,4},{16,8},{20,12},{24,16},{28,20},{32,24... | collective-permute-start | bytes 614408 | tf_op jit(solution)/shard_map/ppermute | solution.py:333
  8.2 53.1 %collective-permute-start.1 = (bf16[2,400,128]{2,1,0:T(8,128)(2,1)S(1)}, bf16[2,400,128]{2,1,0:T(8,128)(2,1)S(1)}, u32[]{:S(2)}, u32[]{:S(2)}) collective-permute-start(bf16[2,400,128]{2,1,0:T(8,128)(2,1)S(1)} %pad_maximum_fusion), channel_id=1, source_target_pairs={{0,8},{4,12},{8,16},{12,20},{16,24},{20,28},{24,32},{28,36},{32,40... | collective-permute-start | bytes 614408 | tf_op jit(solution)/shard_map/ppermute | solution.py:333
  9.6 55.8 %collective-permute-start.8 = (bf16[400,128]{1,0:T(8,128)(2,1)S(1)}, bf16[400,128]{1,0:T(8,128)(2,1)S(1)}, u32[]{:S(2)}, u32[]{:S(2)}) collective-permute-start(bf16[400,128]{1,0:T(8,128)(2,1)S(1)} %copy-done.3), channel_id=1, source_target_pairs={{0,240},{4,20},{8,248},{12,28},{16,0},{20,36},{24,8},{28,44},{32,1... | collective-permute-start | bytes 307208 | tf_op jit(solution)/shard_map/ppermute | solution.py:333
  21.7 83.8 %collective-permute-start.6 = (bf16[2,400,128]{2,1,0:T(8,128)(2,1)S(1)}, bf16[2,400,128]{2,1,0:T(8,128)(2,1)S(1)}, u32[]{:S(2)}, u32[]{:S(2)}) collective-permute-start(bf16[2,400,128]{2,1,0:T(8,128)(2,1)S(1)} %attend_near.8), channel_id=1, source_target_pairs={{0,240},{4,20},{8,248},{12,28},{16,0},{20,36},{24,8},{28,44},{32,1... | collective-permute-start | bytes 614408 | tf_op jit(solution)/shard_map/ppermute | solution.py:333
  58.9 46.6 %collective-permute-start.4 = (bf16[2,400,128]{2,1,0:T(8,128)(2,1)S(1)}, bf16[2,400,128]{2,1,0:T(8,128)(2,1)S(1)}, u32[]{:S(2)}, u32[]{:S(2)}) collective-permute-start(bf16[2,400,128]{2,1,0:T(8,128)(2,1)S(1)} %attend_near.7), channel_id=1, source_target_pairs={{0,8},{4,12},{8,16},{12,20},{16,24},{20,28},{24,32},{28,36},{32,40... | collective-permute-start | bytes 614408 | tf_op jit(solution)/shard_map/ppermute | solution.py:333
  63.8 41.7 %collective-permute-start.2 = (bf16[2,400,128]{2,1,0:T(8,128)(2,1)S(1)}, bf16[2,400,128]{2,1,0:T(8,128)(2,1)S(1)}, u32[]{:S(2)}, u32[]{:S(2)}) collective-permute-start(bf16[2,400,128]{2,1,0:T(8,128)(2,1)S(1)} %attend_near.6), channel_id=1, source_target_pairs={{0,248},{4,252},{8,0},{12,4},{16,8},{20,12},{24,16},{28,20},{32,24... | collective-permute-start | bytes 614408 | tf_op jit(solution)/shard_map/ppermute | solution.py:333
  67.8 42.6 %copy-start.2 = (bf16[384,1536]{1,0:T(8,128)(2,1)S(1)}, bf16[384,1536]{1,0:T(8,128)(2,1)}, u32[]{:S(2)}) copy-start(bf16[384,1536]{1,0:T(8,128)(2,1)} %refs_5_.1) | copy-start | bytes 3538948
  67.8 38.0 %collective-permute-start.9 = (bf16[1,400,128]{2,1,0:T(8,128)(2,1)S(1)}, bf16[1,400,128]{2,1,0:T(8,128)(2,1)S(1)}, u32[]{:S(2)}, u32[]{:S(2)}) collective-permute-start(bf16[1,400,128]{2,1,0:T(8,128)(2,1)S(1)} %attend_near.9), channel_id=1, source_target_pairs={{0,16},{4,244},{8,24},{12,252},{16,32},{20,4},{24,40},{28,12},{32,... | collective-permute-start | bytes 307208 | tf_op jit(solution)/shard_map/ppermute | solution.py:333
  105.6 4.7 %collective-permute-start.7 = (bf16[400,128]{1,0:T(8,128)(2,1)S(1)}, bf16[400,128]{1,0:T(8,128)(2,1)S(1)}, u32[]{:S(2)}, u32[]{:S(2)}) collective-permute-start(bf16[400,128]{1,0:T(8,128)(2,1)S(1)} %merge_other.1), channel_id=1, source_target_pairs={{0,4},{4,0},{8,12},{12,8},{16,20},{20,16},{24,28},{28,24},{32,36},... | collective-permute-start | bytes 307208 | tf_op jit(solution)/shard_map/ppermute | solution.py:337
  111.0 56.0 %collective-permute-start.10 = (bf16[2,128,384]{2,1,0:T(8,128)(2,1)S(1)}, bf16[2,128,384]{2,1,0:T(8,128)(2,1)S(1)}, u32[]{:S(2)}, u32[]{:S(2)}) collective-permute-start(bf16[2,128,384]{2,1,0:T(8,128)(2,1)S(1)} %get-tuple-element.12), channel_id=1, source_target_pairs={{0,1},{1,0},{2,3},{3,2},{4,5},{5,4},{6,7},{7,6},{8,9},{9,8},{10,11... | collective-permute-start | bytes 589832 | tf_op jit(solution)/shard_map/ppermute | solution.py:337
  167.0 6.7 %collective-permute-start.11 = (bf16[128,384]{1,0:T(8,128)(2,1)S(1)}, bf16[128,384]{1,0:T(8,128)(2,1)S(1)}, u32[]{:S(2)}, u32[]{:S(2)}) collective-permute-start(bf16[128,384]{1,0:T(8,128)(2,1)S(1)} %fusion.1), channel_id=1, source_target_pairs={{0,2},{1,3},{2,0},{3,1},{4,6},{5,7},{6,4},{7,5},{8,10},{9,11},{10,... | collective-permute-start | bytes 294920 | tf_op jit(solution)/shard_map/ppermute | solution.py:337
